TPU v7x, 256 devices: a whole 4x4x8 slice. The times are simulated.
256 devices in a mesh: row: 16 (over z, y_lo), col: 16 (over y_hi, x, core).
Axes of the slice: x: 4, y: 4 (y_hi: 2, y_lo: 2; y = y_hi * 2 + y_lo), z: 8, core: 2. Of those that a mesh axis runs over, the one named last changes fastest.
Arguments:
- rho_re: float32 [4096, 4096], P('row', 'col'), may hold values from -6 to 6
- rho_im: float32 [4096, 4096], P('row', 'col'), may hold values from -6 to 6
- diag_re: bfloat16 [16, 256, 256], P('col'), may hold values from -0.21875 to 0.21875
- diag_im: bfloat16 [16, 256, 256], P('col'), may hold values from -0.21875 to 0.21875
- coupling_re: bfloat16 [16, 256, 256], P('col'), may hold values from -0.21875 to 0.21875
- coupling_im: bfloat16 [16, 256, 256], P('col'), may hold values from -0.21875 to 0.21875
- inject_re: bfloat16 [16, 256, 256], P('col'), may hold values from -0.375 to 0.375
- inject_im: bfloat16 [16, 256, 256], P('col'), may hold values from -0.375 to 0.375
- dephasing: float32 [4096], replicated, may hold values from 0.2 to 2
- lead_slice: int32 [4], replicated, may hold values from 0 to 15
- lead_slot: int32 [4], replicated, may hold values from 0 to 15
Outputs:
- prop_re: float32 [4096, 4096], P('row', 'col')
- prop_im: float32 [4096, 4096], P('row', 'col')
Inputs may be any that keep to these rules, and one draw needn't show every extreme that they name: lead_slice holds slice numbers of the window, 0 to 15; several contacts may share a slice. lead_slot holds numbers of stored injection blocks, 0 to 15; several contacts may share a block.
All inputs are finite; a program needn't handle non-finite values.
Results may differ from a plain program's by a relative error of at most 0.0032.
Values may be sent and summed in bfloat16 or wider, within the bound.
A program may use at most 64 MiB of HBM per device.

v0:
```python
import jax
import jax.numpy as jnp
from jax import lax
from jax.sharding import PartitionSpec as P

S = 256
LEADS = 4


step_scale = 0.25
coeff_zero = 0.7652
coeff_one = 0.8801
coeff_two = 0.2298


def shifted(value, axis, by):
    peers = lax.axis_size(axis)
    pairs = [(i, i + by) for i in range(peers) if 0 <= i + by < peers]
    return lax.ppermute(value, axis, pairs)


def spread(value, axis, source):
    kept = jnp.where(lax.axis_index(axis) == source, value, 0).astype(value.dtype)
    return lax.psum(kept, axis)


def extended_2(cells, sides, width):
    for axis, dim in sides:
        count = lax.axis_size(axis)
        ends = count - 1
        head = lax.slice_in_dim(cells, 0, width, axis=dim)
        tail = lax.slice_in_dim(cells, cells.shape[dim] - width, cells.shape[dim], axis=dim)
        cells = jnp.concatenate(
            [
                lax.ppermute(tail, axis, [(i, (i + 1) % count) for i in range(ends)]),
                cells,
                lax.ppermute(head, axis, [((i + 1) % count, i) for i in range(ends)]),
            ],
            axis=dim,
        )
    return cells


def hermitian(part_re, part_im):
    sym_re = 0.5 * (part_re.astype(jnp.float32) + jnp.swapaxes(part_re, -1, -2).astype(jnp.float32))
    sym_im = 0.5 * (part_im.astype(jnp.float32) - jnp.swapaxes(part_im, -1, -2).astype(jnp.float32))
    return (sym_re.astype(jnp.bfloat16), sym_im.astype(jnp.bfloat16))


def product(first, second):
    return jnp.dot(first, second, preferred_element_type=jnp.float32)


def product_first_t(first, second):
    return lax.dot_general(
        first, second, (((0,), (0,)), ((), ())), preferred_element_type=jnp.float32
    )


def product_second_t(first, second):
    return lax.dot_general(
        first, second, (((1,), (1,)), ((), ())), preferred_element_type=jnp.float32
    )


def left_times(block_re, block_im, data_re, data_im):
    return (
        product(block_re, data_re) - product(block_im, data_im),
        product(block_re, data_im) + product(block_im, data_re),
    )


def left_adjoint(block_re, block_im, data_re, data_im):
    return (
        product_first_t(block_re, data_re) + product_first_t(block_im, data_im),
        product_first_t(block_re, data_im) - product_first_t(block_im, data_re),
    )


def right_times(data_re, data_im, block_re, block_im):
    return (
        product(data_re, block_re) - product(data_im, block_im),
        product(data_re, block_im) + product(data_im, block_re),
    )


def right_adjoint(data_re, data_im, block_re, block_im):
    return (
        product_second_t(data_re, block_re) + product_second_t(data_im, block_im),
        product_second_t(data_im, block_re) - product_second_t(data_re, block_im),
    )


def shards(
    rho_re,
    rho_im,
    diag_re,
    diag_im,
    coupling_re,
    coupling_im,
    inject_re,
    inject_im,
    dephasing,
    lead_slice,
    lead_slot,
):
    row_count = rho_re.shape[0]
    column_count = rho_re.shape[1]
    row_slices = row_count // S
    column_slices = column_count // S
    row_first = lax.axis_index("row") * row_slices
    column_first = lax.axis_index("col") * column_slices
    local_re, local_im = hermitian(diag_re, diag_im)
    last_pair = jnp.stack([coupling_re[-1], coupling_im[-1]])
    before_pair = shifted(last_pair, "col", 1)
    extended = jnp.stack(
        [
            jnp.concatenate([before_pair[0][None], coupling_re], axis=0),
            jnp.concatenate([before_pair[1][None], coupling_im], axis=0),
        ]
    )
    local_pair = jnp.stack([local_re, local_im])
    packed = jnp.concatenate([local_pair, extended], axis=1)
    root_index = row_first // column_slices
    received = spread(packed, "col", root_index)
    row_diag = received[:, :column_slices]
    row_ext = received[:, column_slices:]
    per_device = inject_re.shape[0]
    stored = jnp.stack([inject_re, inject_im])
    lead_pairs = []
    for lead_index in range(LEADS):
        slot_index = lead_slot[lead_index]
        fetched = spread(stored, "col", slot_index // per_device)
        lead_pairs.append(
            lax.dynamic_index_in_dim(fetched, slot_index % per_device, axis=1, keepdims=False)
        )
    gamma_rows = lax.dynamic_slice_in_dim(dephasing, row_first * S, row_count)
    gamma_columns = lax.dynamic_slice_in_dim(dephasing, column_first * S, column_count)
    global_rows = row_first * S + lax.iota(jnp.int32, row_count)
    global_columns = column_first * S + lax.iota(jnp.int32, column_count)
    off_diag = (global_rows[:, None] != global_columns[None, :]).astype(jnp.float32)
    rate = 0.5 * (gamma_rows[:, None] + gamma_columns[None, :]) * off_diag

    def generator(field_re, field_im):
        stacked = jnp.stack([field_re, field_im]).astype(jnp.bfloat16)
        by_rows = extended_2(stacked, (("row", 1),), S)
        by_columns = extended_2(stacked, (("col", 2),), S)
        upper_rows = by_rows[:, 0:S]
        middle_rows = by_rows[:, S : 2 * S]
        lower_rows = by_rows[:, 2 * S : 3 * S]
        term_a = left_times(row_ext[0, 0], row_ext[1, 0], upper_rows[0], upper_rows[1])
        term_b = left_times(row_diag[0, 0], row_diag[1, 0], middle_rows[0], middle_rows[1])
        term_c = left_adjoint(row_ext[0, 1], row_ext[1, 1], lower_rows[0], lower_rows[1])
        left_list_re = term_a[0] + term_b[0] + term_c[0]
        left_list_im = term_a[1] + term_b[1] + term_c[1]
        prior_cols = by_columns[:, :, 0:S]
        middle_cols = by_columns[:, :, S : 2 * S]
        later_cols = by_columns[:, :, 2 * S : 3 * S]
        term_d = right_adjoint(prior_cols[0], prior_cols[1], extended[0, 0], extended[1, 0])
        term_e = right_times(middle_cols[0], middle_cols[1], local_re[0], local_im[0])
        term_f = right_times(later_cols[0], later_cols[1], extended[0, 1], extended[1, 1])
        right_list_re = term_d[0] + term_e[0] + term_f[0]
        right_list_im = term_d[1] + term_e[1] + term_f[1]
        gen_re = left_list_im - right_list_im - rate * field_re
        gen_im = -(left_list_re - right_list_re) - rate * field_im
        for lead_index in range(LEADS):
            kblock = lead_pairs[lead_index]
            row_local = lead_slice[lead_index] - row_first
            column_local = lead_slice[lead_index] - column_first

            def row_term(values, kblock=kblock, row_local=row_local):
                made_re, made_im = left_times(kblock[0], kblock[1], stacked[0], stacked[1])
                new_re = values[0] - made_re
                new_im = values[1] - made_im
                return (new_re, new_im)

            def column_term(values, kblock=kblock, column_local=column_local):
                made_re, made_im = right_adjoint(stacked[0], stacked[1], kblock[0], kblock[1])
                new_re = values[0] - made_re
                new_im = values[1] - made_im
                return (new_re, new_im)

            def unchanged(values):
                return (values[0], values[1])

            row_owned = (row_local >= 0) & (row_local < row_slices)
            gen_re, gen_im = lax.cond(row_owned, row_term, unchanged, (gen_re, gen_im))
            column_owned = (column_local >= 0) & (column_local < column_slices)
            gen_re, gen_im = lax.cond(column_owned, column_term, unchanged, (gen_re, gen_im))
        return (step_scale * gen_re, step_scale * gen_im)

    one_re, one_im = generator(rho_re, rho_im)
    next_re, next_im = generator(one_re, one_im)
    two_re = 2.0 * next_re - rho_re
    two_im = 2.0 * next_im - rho_im
    prop_re = coeff_zero * rho_re + coeff_one * one_re + coeff_two * two_re
    prop_im = coeff_zero * rho_im + coeff_one * one_im + coeff_two * two_im
    return (prop_re, prop_im)


def solution(mesh):
    return jax.shard_map(
        shards,
        mesh=mesh,
        in_specs=(
            P("row", "col"),
            P("row", "col"),
            P("col", None, None),
            P("col", None, None),
            P("col", None, None),
            P("col", None, None),
            P("col", None, None),
            P("col", None, None),
            P(),
            P(),
            P(),
        ),
        out_specs=(P("row", "col"), P("row", "col")),
        check_vma=False,
    )
```

profile of v0, /device:TPU:1, one launch (start us, length us, event | category | flops | bytes accessed | tf_op | source)
XLA Modules:
  0.0 244.2 jit_solution(11289890034513888756)
XLA Ops:
  7.2 1.0 convert_bitcast_fusion.1
  8.3 4.6 %collective-permute-start.3 = (bf16[2,256,256]{2,1,0:T(8,128)(2,1)S(1)}, bf16[2,256,256]{2,1,0:T(8,128)(2,1)S(1)}, u32[]{:S(2)}, u32[]{:S(2)}) collective-permute-start(bf16[2,256,256]{2,1,0:T(8,128)(2,1)S(1)} %pad_maximum_fusion.2), channel_id=1, source_target_pairs={{0,1},{1,2},{2,3},{3,4},{4,5},{5,6},{6,7},{7,8},{8,9},{9,10},{10,1... | collective-permute-start | bytes 786440 | tf_op jit(solution)/shard_map/ppermute | solution.py:35
  13.0 1.9 collective-permute-start.4
  14.9 1.3 collective-permute-start.2
  16.2 4.0 %collective-permute-start.1 = (bf16[2,256,256]{2,1,0:T(8,128)(2,1)S(1)}, bf16[2,256,256]{2,1,0:T(8,128)(2,1)S(1)}, u32[]{:S(2)}, u32[]{:S(2)}) collective-permute-start(bf16[2,256,256]{2,1,0:T(8,128)(2,1)S(1)} %pad_maximum_fusion.2), channel_id=1, source_target_pairs={{0,16},{16,32},{32,48},{48,64},{64,80},{80,96},{96,112},{112,128},... | collective-permute-start | bytes 786440 | tf_op jit(solution)/shard_map/ppermute | solution.py:35
  20.3 4.3 %collective-permute-start = (bf16[2,256,256]{2,1,0:T(8,128)(2,1)S(1)}, bf16[2,256,256]{2,1,0:T(8,128)(2,1)}, u32[]{:S(2)}, u32[]{:S(2)}) collective-permute-start(bf16[2,256,256]{2,1,0:T(8,128)(2,1)S(1)} %pad_maximum_fusion.1), channel_id=1, source_target_pairs={{0,1},{1,2},{2,3},{3,4},{4,5},{5,6},{6,7},{7,8},{8,9},{9,10},{10,1... | collective-permute-start | bytes 786440 | tf_op jit(solution)/shard_map/ppermute | solution.py:19
  26.2 0.9 copy-done.18
  32.3 1.0 select_bitcast_fusion
  33.3 0.8 fusion.386
  39.4 1.0 fusion.385
  40.5 1.0 maximum_select_fusion
  42.4 1.1 fusion.372
  43.5 1.1 fusion.371
  44.9 1.8 fusion.334
  46.9 1.8 fusion.330
  48.7 147.1 %all-reduce.3.cloned.1.call-done = (bf16[2,3,256,256]{3,2,1,0:T(8,128)(2,1)}, bf16[2,256,256]{2,1,0:T(8,128)(2,1)}, bf16[2,256,256]{2,1,0:T(8,128)(2,1)}, bf16[2...) async-done(((bf16[2,3,256,256]{3,2,1,0:T(8,128)(2,1)}, bf16[2,256,256]{2,1,0:T(8,128)(2,1)}, bf16[2,256,256]{2,1,0:T(8,128)(2,1)}, bf16[2,256,256]{2,1,0:T(8,128)(2,1)}, ...) | async-done | bytes 1835024 | tf_op jit(solution)/shard_map/psum | solution.py:24
  195.8 1.2 fusion.384
  197.0 1.1 fusion.383
  198.3 1.1 fusion.368
  199.4 1.1 fusion.367
  201.1 1.1 convolution_subtract_fusion.27
  202.3 1.2 convolution_add_fusion.24
  205.4 0.9 copy-done.2
  207.2 0.9 copy-done.1
  208.1 0.9 copy-done
  209.2 3.1 %collective-permute-start.8 = (bf16[2,256,256]{2,1,0:T(8,128)(2,1)S(1)}, bf16[2,256,256]{2,1,0:T(8,128)(2,1)S(1)}, u32[]{:S(2)}, u32[]{:S(2)}) collective-permute-start(bf16[2,256,256]{2,1,0:T(8,128)(2,1)S(1)} %pad_maximum_fusion.4), channel_id=1, source_target_pairs={{1,0},{2,1},{3,2},{4,3},{5,4},{6,5},{7,6},{8,7},{9,8},{10,9},{11,1... | collective-permute-start | bytes 786440 | tf_op jit(solution)/shard_map/ppermute | solution.py:37
  212.3 2.5 %collective-permute-start.7 = (bf16[2,256,256]{2,1,0:T(8,128)(2,1)S(1)}, bf16[2,256,256]{2,1,0:T(8,128)(2,1)S(1)}, u32[]{:S(2)}, u32[]{:S(2)}) collective-permute-start(bf16[2,256,256]{2,1,0:T(8,128)(2,1)S(1)} %pad_maximum_fusion.4), channel_id=1, source_target_pairs={{0,1},{1,2},{2,3},{3,4},{4,5},{5,6},{6,7},{7,8},{8,9},{9,10},{10,1... | collective-permute-start | bytes 786440 | tf_op jit(solution)/shard_map/ppermute | solution.py:35
  214.8 1.3 collective-permute-start.6
  216.1 4.0 %collective-permute-start.5 = (bf16[2,256,256]{2,1,0:T(8,128)(2,1)S(1)}, bf16[2,256,256]{2,1,0:T(8,128)(2,1)S(1)}, u32[]{:S(2)}, u32[]{:S(2)}) collective-permute-start(bf16[2,256,256]{2,1,0:T(8,128)(2,1)S(1)} %pad_maximum_fusion.4), channel_id=1, source_target_pairs={{0,16},{16,32},{32,48},{48,64},{64,80},{80,96},{96,112},{112,128},... | collective-permute-start | bytes 786440 | tf_op jit(solution)/shard_map/ppermute | solution.py:35
  222.5 5.0 %collective-permute-done.6 = bf16[2,256,256]{2,1,0:T(8,128)(2,1)S(1)} collective-permute-done((bf16[2,256,256]{2,1,0:T(8,128)(2,1)S(1)}, bf16[2,256,256]{2,1,0:T(8,128)(2,1)S(1)}, u32[]{:S(2)}, u32[]{:S(2)}) %collective-permute-start.6) | collective-permute-done | bytes 262176 | tf_op jit(solution)/shard_map/ppermute | solution.py:37
  227.9 3.6 %collective-permute-done.5 = bf16[2,256,256]{2,1,0:T(8,128)(2,1)S(1)} collective-permute-done((bf16[2,256,256]{2,1,0:T(8,128)(2,1)S(1)}, bf16[2,256,256]{2,1,0:T(8,128)(2,1)S(1)}, u32[]{:S(2)}, u32[]{:S(2)}) %collective-permute-start.5) | collective-permute-done | bytes 262176 | tf_op jit(solution)/shard_map/ppermute | solution.py:35
  234.7 0.9 copy-done.6
  (130 shorter events, 18.6 us)
Async XLA Ops:
  7.2 1.1 copy-start.5
  7.2 188.6 %all-reduce.3.cloned.1.call-start = ((), (), s32[]{:S(2)}) async-start(), calls=%async_computation | async-start | bytes 3670016 | tf_op jit(solution)/shard_map/psum | solution.py:24
  8.3 12.0 %copy-start.13 = (bf16[1,256,256]{2,1,0:T(8,128)(2,1)S(1)}, bf16[1,256,256]{2,1,0:T(8,128)(2,1)}, u32[]{:S(2)}) copy-start(bf16[1,256,256]{2,1,0:T(8,128)(2,1)} %param.48) | copy-start | bytes 393220
  8.3 12.0 %copy-start.14 = (bf16[1,256,256]{2,1,0:T(8,128)(2,1)S(1)}, bf16[1,256,256]{2,1,0:T(8,128)(2,1)}, u32[]{:S(2)}) copy-start(bf16[1,256,256]{2,1,0:T(8,128)(2,1)} %param.47) | copy-start | bytes 393220
  8.3 33.2 %collective-permute-start.3 = (bf16[2,256,256]{2,1,0:T(8,128)(2,1)S(1)}, bf16[2,256,256]{2,1,0:T(8,128)(2,1)S(1)}, u32[]{:S(2)}, u32[]{:S(2)}) collective-permute-start(bf16[2,256,256]{2,1,0:T(8,128)(2,1)S(1)} %pad_maximum_fusion.2), channel_id=1, source_target_pairs={{0,1},{1,2},{2,3},{3,4},{4,5},{5,6},{6,7},{7,8},{8,9},{9,10},{10,1... | collective-permute-start | bytes 786440 | tf_op jit(solution)/shard_map/ppermute | solution.py:35
  13.0 29.4 %collective-permute-start.4 = (bf16[2,256,256]{2,1,0:T(8,128)(2,1)S(1)}, bf16[2,256,256]{2,1,0:T(8,128)(2,1)}, u32[]{:S(2)}, u32[]{:S(2)}) collective-permute-start(bf16[2,256,256]{2,1,0:T(8,128)(2,1)S(1)} %pad_maximum_fusion.2), channel_id=1, source_target_pairs={{1,0},{2,1},{3,2},{4,3},{5,4},{6,5},{7,6},{8,7},{9,8},{10,9},{11,1... | collective-permute-start | bytes 786440 | tf_op jit(solution)/shard_map/ppermute | solution.py:37
  14.9 183.4 %collective-permute-start.2 = (bf16[2,256,256]{2,1,0:T(8,128)(2,1)S(1)}, bf16[2,256,256]{2,1,0:T(8,128)(2,1)}, u32[]{:S(2)}, u32[]{:S(2)}) collective-permute-start(bf16[2,256,256]{2,1,0:T(8,128)(2,1)S(1)} %pad_maximum_fusion.2), channel_id=1, source_target_pairs={{16,0},{32,16},{48,32},{64,48},{80,64},{96,80},{112,96},{128,112},... | collective-permute-start | bytes 786440 | tf_op jit(solution)/shard_map/ppermute | solution.py:37
  16.2 184.5 %collective-permute-start.1 = (bf16[2,256,256]{2,1,0:T(8,128)(2,1)S(1)}, bf16[2,256,256]{2,1,0:T(8,128)(2,1)S(1)}, u32[]{:S(2)}, u32[]{:S(2)}) collective-permute-start(bf16[2,256,256]{2,1,0:T(8,128)(2,1)S(1)} %pad_maximum_fusion.2), channel_id=1, source_target_pairs={{0,16},{16,32},{32,48},{48,64},{64,80},{80,96},{96,112},{112,128},... | collective-permute-start | bytes 786440 | tf_op jit(solution)/shard_map/ppermute | solution.py:35
  20.3 4.4 %copy-start.7 = (f32[256,256]{1,0:T(8,128)S(1)}, f32[256,256]{1,0:T(8,128)}, u32[]{:S(2)}) copy-start(f32[256,256]{1,0:T(8,128)} %param.44) | copy-start | bytes 786436
  20.3 19.1 %collective-permute-start = (bf16[2,256,256]{2,1,0:T(8,128)(2,1)S(1)}, bf16[2,256,256]{2,1,0:T(8,128)(2,1)}, u32[]{:S(2)}, u32[]{:S(2)}) collective-permute-start(bf16[2,256,256]{2,1,0:T(8,128)(2,1)S(1)} %pad_maximum_fusion.1), channel_id=1, source_target_pairs={{0,1},{1,2},{2,3},{3,4},{4,5},{5,6},{6,7},{7,8},{8,9},{9,10},{10,1... | collective-permute-start | bytes 786440 | tf_op jit(solution)/shard_map/ppermute | solution.py:19
  24.7 0.7 copy-start.19
  24.7 1.3 copy-start.17
  26.2 0.9 copy-start.18
  27.3 0.7 copy-start.20
  31.4 0.9 copy-start.15
  31.4 1.0 copy-start.16
  41.5 0.7 copy-start.11
  43.5 1.1 copy-start.12
  195.8 2.3 copy-start.4
  202.3 1.2 copy-start.9
  203.5 1.0 copy-start.10
  204.4 0.9 copy-start.3
  205.4 0.9 copy-start.2
  207.1 1.0 copy-start.1
  208.1 0.9 copy-start
  209.2 12.4 %collective-permute-start.8 = (bf16[2,256,256]{2,1,0:T(8,128)(2,1)S(1)}, bf16[2,256,256]{2,1,0:T(8,128)(2,1)S(1)}, u32[]{:S(2)}, u32[]{:S(2)}) collective-permute-start(bf16[2,256,256]{2,1,0:T(8,128)(2,1)S(1)} %pad_maximum_fusion.4), channel_id=1, source_target_pairs={{1,0},{2,1},{3,2},{4,3},{5,4},{6,5},{7,6},{8,7},{9,8},{10,9},{11,1... | collective-permute-start | bytes 786440 | tf_op jit(solution)/shard_map/ppermute | solution.py:37
  212.3 9.8 %collective-permute-start.7 = (bf16[2,256,256]{2,1,0:T(8,128)(2,1)S(1)}, bf16[2,256,256]{2,1,0:T(8,128)(2,1)S(1)}, u32[]{:S(2)}, u32[]{:S(2)}) collective-permute-start(bf16[2,256,256]{2,1,0:T(8,128)(2,1)S(1)} %pad_maximum_fusion.4), channel_id=1, source_target_pairs={{0,1},{1,2},{2,3},{3,4},{4,5},{5,6},{6,7},{7,8},{8,9},{9,10},{10,1... | collective-permute-start | bytes 786440 | tf_op jit(solution)/shard_map/ppermute | solution.py:35
  214.8 12.7 %collective-permute-start.6 = (bf16[2,256,256]{2,1,0:T(8,128)(2,1)S(1)}, bf16[2,256,256]{2,1,0:T(8,128)(2,1)S(1)}, u32[]{:S(2)}, u32[]{:S(2)}) collective-permute-start(bf16[2,256,256]{2,1,0:T(8,128)(2,1)S(1)} %pad_maximum_fusion.4), channel_id=1, source_target_pairs={{16,0},{32,16},{48,32},{64,48},{80,64},{96,80},{112,96},{128,112},... | collective-permute-start | bytes 786440 | tf_op jit(solution)/shard_map/ppermute | solution.py:37
  216.1 15.5 %collective-permute-start.5 = (bf16[2,256,256]{2,1,0:T(8,128)(2,1)S(1)}, bf16[2,256,256]{2,1,0:T(8,128)(2,1)S(1)}, u32[]{:S(2)}, u32[]{:S(2)}) collective-permute-start(bf16[2,256,256]{2,1,0:T(8,128)(2,1)S(1)} %pad_maximum_fusion.4), channel_id=1, source_target_pairs={{0,16},{16,32},{32,48},{48,64},{64,80},{80,96},{96,112},{112,128},... | collective-permute-start | bytes 786440 | tf_op jit(solution)/shard_map/ppermute | solution.py:35
  234.7 1.0 copy-start.6
  235.6 0.9 copy-start.8
Sparse Core Ops, SparseCore 0:
  41.6 154.1 all-reduce.2
where the time goes:
time: 245 us; the launch traced here: 244 us
  waiting for transfers between devices  156 us (64%)
  starting transfers between devices  27.1 us (11%)
  between operations  22.4 us (9%)
  matrix products  21.8 us (9%)
  local copies, waits for them, and re-layouts  12.2 us (5%)
  other arithmetic  4.83 us (2%)
    psum x1, waiting for transfers between devices, spread(): return lax.psum(kept, axis)  147 us
    ppermute x4, starting transfers between devices, extended_2(): lax.ppermute(tail, axis, [(i, (i + 1) % count) for i in range(ends)])  15.1 us
    dot_general x40, matrix products, product(): return jnp.dot(first, second, preferred_element_type=jnp.float32)  14.6 us
    unnamed x44, local copies, waits for them, and re-layouts  8.89 us
    ppermute x4, starting transfers between devices, extended_2(): lax.ppermute(head, axis, [((i + 1) % count, i) for i in range(ends)])  7.6 us
    dot_general x8, matrix products, product_first_t(): lax.dot_general(first, second, (((0,), (0,)), ((), ())), preferred_elemen...  5.45 us
    ppermute x4, waiting for transfers between devices, extended_2(): lax.ppermute(head, axis, [((i + 1) % count, i) for i in range(ends)])  5.01 us
  transfers between devices with their start and end apart: 10, of which 3 were waited for; matrix products, arithmetic and copies ran while one was open for 8% of the time, Pallas kernels for 0%

commit v1 on v0

v1 whole, which is shorter than its diff:
```python
import jax
import jax.numpy as jnp
from jax import lax
from jax.experimental import pallas as pl
from jax.experimental.pallas import tpu as pltpu
from jax.sharding import PartitionSpec as P

S = 256
LEADS = 4
PIECE = 16

step_scale = 0.25
coeff_zero = 0.7652
coeff_one = 0.8801
coeff_two = 0.2298

BF = jnp.bfloat16
F32 = jnp.float32
MESH = pl.DeviceIdType.MESH


def nn(a, b):
    return jnp.dot(a, b, preferred_element_type=F32)


def nt(a, b):
    return lax.dot_general(a, b, (((1,), (1,)), ((), ())), preferred_element_type=F32)


def pick(key, table):
    out = jnp.int32(table[-1])
    for i in range(len(table) - 1):
        out = jnp.where(key == i, jnp.int32(table[i]), out)
    return out


STEP_OF = ((1, 0, 2, 4, 4, 4, 4, 3), (3, 1, 4, 4, 4, 4, 2, 0))
OFF_OF = ((1, 0, 2, 7), (7, 1, 6, 0))


def kernel(
    rho_re, rho_im, diag_re, diag_im, coup_re, coup_im, inj_re, inj_im, deph,
    lead_slice, lead_slot,
    out_re, out_im,
    field, part, far, right, q_out, q_in, kmine, kall, dmat, lpiece, lcol, lrow, crow, cprev,
    l_part, l_far, rate, phi,
    y_send, y_recv, z_send, z_recv, c_send, c_recv, q_send, q_recv,
    k_send, k_recv, a_send, a_recv, b_send, b_recv, h_send, h_recv, s_send, s_recv,
):
    r = lax.axis_index("row")
    c = lax.axis_index("col")
    core = c % 2
    y_lo = r % 2
    partner = r + 1 - 2 * y_lo
    relay = (r + 2 - 4 * y_lo + 16) % 16
    relay_from = (r - 2 + 4 * y_lo + 16) % 16
    c_next = (c + 1) % 16
    c_prior = (c + 15) % 16
    c_mate = c + 1 - 2 * core

    def dev(a, b):
        return {"row": a, "col": b}

    zr, xc, hc = r // 2, (c // 2) % 4, c // 8
    sources = []
    for j in range(2):
        q = (r + 16 - j) % 16
        step = (xc + 4 - (q // 2) % 4) % 4
        zp = (zr + pick(step, OFF_OF[j])) % 8
        yp = jnp.where(hc == q // 8, y_lo, 1 - y_lo)
        sources.append((2 * zp + yp, q))
    targets = []
    for j in range(2):
        row_to = (c + j) % 16
        step = pick((r // 2 + 8 - row_to // 2) % 8, STEP_OF[j])
        x_to = ((c // 2) % 4 + step) % 4
        h_to = jnp.where(y_lo == row_to % 2, c // 8, 1 - c // 8)
        targets.append((step < 4, row_to, 8 * h_to + 2 * x_to))

    barrier = pltpu.get_barrier_semaphore()

    def greet(a, b):
        pl.semaphore_signal(barrier, inc=1, device_id=dev(a, b), device_id_type=MESH)

    greet(partner, c)
    greet(relay_from, c)
    greet(r, c_next)
    greet(r, c_prior)
    greet(r, c_mate)
    for p, q in sources:
        greet(p, q)

    @pl.loop(1, 16)
    def _(i):
        greet(r, (c + i) % 16)
        greet((r + i) % 16, c)

    @pl.loop(0, 16)
    def _(i):
        @pl.when(jnp.logical_or(i != r, c != r))
        def _():
            greet(i, r)

    field[0] = rho_re[...].astype(BF)
    field[1] = rho_im[...].astype(BF)
    rows16 = pl.ds(pl.multiple_of(r * PIECE, PIECE), PIECE)
    kmine[0] = inj_re[0, rows16, :]
    kmine[1] = inj_im[0, rows16, :]
    kall[c] = kmine[...]

    own_piece = jnp.where(r == c, 1, 0)
    sends_h = sum(jnp.where(t[0], 2, 0) for t in targets)
    pl.semaphore_wait(barrier, 5 + 30 + 16 - own_piece + sends_h)

    def remote(src, dst, ss, rs, to):
        return pltpu.make_async_remote_copy(
            src_ref=src, dst_ref=dst, send_sem=ss, recv_sem=rs, device_id=to, device_id_type=MESH
        )

    def row_copies(g):
        ys = [remote(field.at[2 * g + i], part.at[2 * g + i], y_send.at[2 * g + i], y_recv.at[2 * g + i], dev(partner, c)) for i in range(2)]
        zs = [remote(part.at[2 * g + i], far.at[2 * g + i], z_send.at[2 * g + i], z_recv.at[2 * g + i], dev(relay, c)) for i in range(2)]
        return ys, zs

    def col_copies(g):
        two = pl.ds(2 * g, 2)
        cs = remote(field.at[two], right.at[two], c_send.at[g], c_recv.at[g], dev(r, c_prior))
        qs = remote(q_out.at[two], q_in.at[two], q_send.at[g], q_recv.at[g], dev(r, c_next))
        return cs, qs

    ys, zs = row_copies(0)
    for y in ys:
        y.start()

    @pl.loop(1, 16)
    def _(i):
        remote(kmine, kall.at[c], k_send, k_recv, dev(r, (c + i) % 16)).start()

    cs, qs = col_copies(0)
    cs.start()
    for j, (on, row_to, col_to) in enumerate(targets):
        land = (crow, cprev)[j]

        @pl.when(on)
        def _():
            remote(coup_re.at[0], land.at[0], h_send.at[2 * j], h_recv.at[j], dev(row_to, col_to)).start()
            remote(coup_im.at[0], land.at[1], h_send.at[2 * j + 1], h_recv.at[j], dev(row_to, col_to + 1)).start()

    def product_right(g):
        fr, fi = field[2 * g], field[2 * g + 1]
        cr, ci = coup_re[0], coup_im[0]
        q_out[2 * g] = (nt(fr, ci) - nt(fi, cr)).astype(BF)
        q_out[2 * g + 1] = (nt(fr, cr) + nt(fi, ci)).astype(BF)

    product_right(0)
    qs.start()

    gr = diag_re[0].astype(F32)
    gi = diag_im[0].astype(F32)
    dmat[0] = (0.5 * (gr + gr.T)).astype(BF)
    dmat[1] = (0.5 * (gi - gi.T)).astype(BF)

    g_rows = deph[pl.ds(pl.multiple_of(r * S, S), S)].reshape(1, S)
    g_cols = deph[pl.ds(pl.multiple_of(c * S, S), S)].reshape(1, S)
    wide = jnp.broadcast_to(g_rows, (S, S)).T + jnp.broadcast_to(g_cols, (S, S))
    ii = lax.broadcasted_iota(jnp.int32, (S, S), 0) + r * S
    jj = lax.broadcasted_iota(jnp.int32, (S, S), 1) + c * S
    rate[...] = jnp.where(ii == jj, 0.0, 0.5 * wide)

    def drain(ref, sem):
        pltpu.make_async_copy(ref, ref, sem).wait()

    drain(kall.at[pl.ds(0, 15)], k_recv)
    sum_re = dmat[1, rows16, :].astype(F32)
    sum_im = -dmat[0, rows16, :].astype(F32)
    for l in range(LEADS):
        block = kall[lead_slot[l]].astype(F32)
        hit = jnp.where(lead_slice[l] == c, 1.0, 0.0)
        sum_re = sum_re - hit * block[0]
        sum_im = sum_im - hit * block[1]
    lpiece[0] = sum_re.astype(BF)
    lpiece[1] = sum_im.astype(BF)
    lcol[r] = lpiece[...]

    @pl.loop(0, 16)
    def _(i):
        @pl.when(jnp.logical_or(r != c, i != c))
        def _():
            remote(lpiece.at[i % 2], lrow.at[i % 2, r], b_send, b_recv, dev(c, i)).start()

    @pl.when(r == c)
    def _():
        lrow[core, r] = lpiece[core]

    @pl.loop(1, 16)
    def _(i):
        remote(lpiece, lcol.at[r], a_send, a_recv, dev((r + i) % 16, c)).start()

    for y, z in zip(ys, zs):
        y.wait_recv()
        z.start()

    shares = []
    for j, land in enumerate((crow, cprev)):
        pltpu.make_async_copy(land.at[0], land.at[0], h_recv.at[j]).wait()
        s = remote(land.at[core], land.at[core], s_send.at[j], s_recv.at[j], dev(r, c_mate))
        s.start()
        shares.append(s)

    @pl.when(r == c)
    def _():
        drain(lrow.at[0, pl.ds(0, 15)], b_recv)

    @pl.when(r != c)
    def _():
        drain(lrow.at[0], b_recv)

    s = remote(lrow.at[core], lrow.at[core], s_send.at[2], s_recv.at[2], dev(r, c_mate))
    s.start()
    shares.append(s)

    shares[0].wait_recv()
    shares[1].wait_recv()
    has_prior = jnp.where(r > 0, 1.0, 0.0).astype(BF)
    minus_prior = jnp.where(r > 0, -1.0, 0.0).astype(BF)
    minus_next = jnp.where(r < 15, -1.0, 0.0).astype(BF)

    def place(to_prior, to_next):
        to_prior[0] = has_prior * cprev[1]
        to_prior[1] = minus_prior * cprev[0]
        to_next[0] = minus_next * crow[1].T
        to_next[1] = minus_next * crow[0].T

    @pl.when(y_lo == 0)
    def _():
        place(l_far, l_part)

    @pl.when(y_lo == 1)
    def _():
        place(l_part, l_far)

    shares[2].wait_recv()
    drain(lcol.at[pl.ds(0, 15)], a_recv)

    def left_add(acc, lr, li, fr, fi):
        return (acc[0] + nn(lr, fr) - nn(li, fi), acc[1] + nn(lr, fi) + nn(li, fr))

    not_last = jnp.where(c < 15, 1.0, 0.0)
    not_first = jnp.where(c > 0, 1.0, 0.0)

    def generator(g, own_re, own_im, zs, cs, qs):
        fr, fi = field[2 * g], field[2 * g + 1]
        acc = (-rate[...] * own_re, -rate[...] * own_im)
        acc = left_add(acc, lrow[0].reshape(S, S), lrow[1].reshape(S, S), fr, fi)
        kr, ki = lcol[:, 0].reshape(S, S), lcol[:, 1].reshape(S, S)
        acc = (acc[0] + nt(fr, kr) + nt(fi, ki), acc[1] + nt(fi, kr) - nt(fr, ki))
        acc = left_add(acc, l_part[0], l_part[1], part[2 * g], part[2 * g + 1])
        cs.wait_recv()
        nr, ni = right[2 * g], right[2 * g + 1]
        cr, ci = coup_re[0], coup_im[0]
        acc = (
            acc[0] - not_last * (nn(nr, ci) + nn(ni, cr)),
            acc[1] + not_last * (nn(nr, cr) - nn(ni, ci)),
        )
        qs.wait_recv()
        acc = (
            acc[0] + not_first * q_in[2 * g].astype(F32),
            acc[1] + not_first * q_in[2 * g + 1].astype(F32),
        )
        for z in zs:
            z.wait_recv()
        acc = left_add(acc, l_far[0], l_far[1], far[2 * g], far[2 * g + 1])
        return step_scale * acc[0], step_scale * acc[1]

    one_re, one_im = generator(0, rho_re[...], rho_im[...], zs, cs, qs)
    field[2] = one_re.astype(BF)
    field[3] = one_im.astype(BF)
    ys2, zs2 = row_copies(1)
    cs2, qs2 = col_copies(1)
    for y in ys2:
        y.start()
    cs2.start()
    phi[0] = one_re
    phi[1] = one_im
    product_right(1)
    qs2.start()
    for y, z in zip(ys2, zs2):
        y.wait_recv()
        z.start()
    two_re, two_im = generator(1, phi[0], phi[1], zs2, cs2, qs2)
    out_re[...] = (coeff_zero - coeff_two) * rho_re[...] + coeff_one * phi[0] + 2.0 * coeff_two * two_re
    out_im[...] = (coeff_zero - coeff_two) * rho_im[...] + coeff_one * phi[1] + 2.0 * coeff_two * two_im

    for copies in (ys, zs, ys2, zs2, (cs, cs2, qs, qs2), shares):
        for one in copies:
            one.wait_send()
    drain(kall.at[pl.ds(0, 15)], k_send)
    drain(lcol.at[pl.ds(0, 15)], a_send)

    @pl.when(r == c)
    def _():
        drain(lrow.at[0, pl.ds(0, 15)], b_send)

    @pl.when(r != c)
    def _():
        drain(lrow.at[0], b_send)

    for j, (on, row_to, col_to) in enumerate(targets):
        @pl.when(on)
        def _():
            pltpu.make_async_copy(coup_re.at[0], coup_re.at[0], h_send.at[2 * j]).wait()
            pltpu.make_async_copy(coup_im.at[0], coup_im.at[0], h_send.at[2 * j + 1]).wait()


def shards(*args):
    vm = pl.BlockSpec(memory_space=pltpu.VMEM)
    sm = pl.BlockSpec(memory_space=pltpu.SMEM)
    dma = pltpu.SemaphoreType.DMA

    def blocks(n):
        return pltpu.VMEM((n, S, S), BF)

    pieces = (16, 2, PIECE, S)
    return pl.pallas_call(
        kernel,
        name="propagate",
        out_shape=[jax.ShapeDtypeStruct((S, S), F32)] * 2,
        in_specs=[vm] * 9 + [sm] * 2,
        out_specs=[vm] * 2,
        scratch_shapes=[
            blocks(4), blocks(4), blocks(4), blocks(4), blocks(4), blocks(4),
            pltpu.VMEM((2, PIECE, S), BF), pltpu.VMEM(pieces, BF), blocks(2),
            pltpu.VMEM((2, PIECE, S), BF), pltpu.VMEM(pieces, BF), pltpu.VMEM((2, 16, PIECE, S), BF),
            blocks(2), blocks(2), blocks(2), blocks(2),
            pltpu.VMEM((S, S), F32), pltpu.VMEM((2, S, S), F32),
            dma((4,)), dma((4,)), dma((4,)), dma((4,)), dma((2,)), dma((2,)), dma((2,)), dma((2,)),
            dma, dma, dma, dma, dma, dma, dma((4,)), dma((2,)), dma((3,)), dma((3,)),
        ],
        compiler_params=pltpu.CompilerParams(
            collective_id=0, has_side_effects=True, vmem_limit_bytes=32 << 20
        ),
    )(*args)


def solution(mesh):
    return jax.shard_map(
        shards,
        mesh=mesh,
        in_specs=(
            P("row", "col"), P("row", "col"),
            P("col", None, None), P("col", None, None), P("col", None, None), P("col", None, None),
            P("col", None, None), P("col", None, None),
            P(), P(), P(),
        ),
        out_specs=(P("row", "col"), P("row", "col")),
        check_vma=False,
    )
```

time: 245 us -> 75.6 us (0.31)
  waiting for transfers between devices: 156 us -> 0 us
  Pallas kernels: 0 us -> 63.9 us
  starting transfers between devices: 27.1 us -> 0 us
  matrix products: 21.8 us -> 0 us
  between operations: 22.4 us -> 0.66 us
  other arithmetic: 4.83 us -> 0 us
    psum x1 -> x0, waiting for transfers between devices: 147 us -> none  [spread(): return lax.psum(kept, axis)]
    pallas_call x0 -> x1, Pallas kernels: none -> 63.9 us  [shards(): pl.pallas_call(kernel, name='propagate', out_shape=[jax.ShapeDtypeStruct(...]
    ppermute x9 -> x0, starting transfers between devices: 27 us -> none  [the longest x4 15.1 us: extended_2(): lax.ppermute(tail, axis, [(i, (i + 1) % count) for i in range(ends)])]
    dot_general x56 -> x0, matrix products: 21.8 us -> none  [the longest x40 14.6 us: product(): return jnp.dot(first, second, preferred_element_type=jnp.float32)]
    ppermute x9 -> x0, waiting for transfers between devices: 8.61 us -> none  [the longest x4 5.01 us: extended_2(): lax.ppermute(head, axis, [((i + 1) % count, i) for i in range(ends)])]
    unnamed x44 -> x24, local copies, waits for them, and re-layouts: 8.89 us -> 10.7 us
  transfers between devices with their start and end apart: 10 -> 0, of which waited for: 3 -> 0; matrix products, arithmetic and copies ran while one was open for 8% -> 0% of each run, Pallas kernels for 0% -> 0%
where the time goes in v1:
time: 75.6 us; the launch traced here: 75.3 us
  Pallas kernels  63.9 us (85%)
  local copies, waits for them, and re-layouts  10.7 us (14%)
    pallas_call x1, Pallas kernels, shards(): pl.pallas_call(kernel, name='propagate', out_shape=[jax.ShapeDtypeStruct(...  63.9 us
    unnamed x24, local copies, waits for them, and re-layouts  10.7 us

profile of v1, /device:TPU:1, one launch (start us, length us, event | category | flops | bytes accessed | tf_op | source)
XLA Modules:
  0.0 75.3 jit_solution(17777391297964630286)
XLA Ops:
  0.6 0.0 copy-start
  0.6 0.9 %copy-done = f32[256,256]{1,0:T(8,128)S(1)} copy-done((f32[256,256]{1,0:T(8,128)S(1)}, f32[256,256]{1,0:T(8,128)}, u32[]{:S(2)}) %copy-start) | copy-done | bytes 262168
  1.6 0.0 copy-start.1
  1.6 0.9 %copy-done.1 = f32[256,256]{1,0:T(8,128)S(1)} copy-done((f32[256,256]{1,0:T(8,128)S(1)}, f32[256,256]{1,0:T(8,128)}, u32[]{:S(2)}) %copy-start.1) | copy-done | bytes 262168
  2.5 0.0 copy-start.2
  2.5 0.9 %copy-done.2 = bf16[1,256,256]{2,1,0:T(8,128)(2,1)S(1)} copy-done((bf16[1,256,256]{2,1,0:T(8,128)(2,1)S(1)}, bf16[1,256,256]{2,1,0:T(8,128)(2,1)}, u32[]{:S(2)}) %copy-start.2) | copy-done | bytes 131096
  3.4 0.0 copy-start.3
  3.4 0.9 %copy-done.3 = bf16[1,256,256]{2,1,0:T(8,128)(2,1)S(1)} copy-done((bf16[1,256,256]{2,1,0:T(8,128)(2,1)S(1)}, bf16[1,256,256]{2,1,0:T(8,128)(2,1)}, u32[]{:S(2)}) %copy-start.3) | copy-done | bytes 131096
  4.3 0.0 copy-start.4
  4.3 0.9 %copy-done.4 = bf16[1,256,256]{2,1,0:T(8,128)(2,1)S(1)} copy-done((bf16[1,256,256]{2,1,0:T(8,128)(2,1)S(1)}, bf16[1,256,256]{2,1,0:T(8,128)(2,1)}, u32[]{:S(2)}) %copy-start.4) | copy-done | bytes 131096
  5.2 0.0 copy-start.5
  5.3 0.9 %copy-done.5 = bf16[1,256,256]{2,1,0:T(8,128)(2,1)S(1)} copy-done((bf16[1,256,256]{2,1,0:T(8,128)(2,1)S(1)}, bf16[1,256,256]{2,1,0:T(8,128)(2,1)}, u32[]{:S(2)}) %copy-start.5) | copy-done | bytes 131096
  6.2 0.0 copy-start.6
  6.2 0.9 %copy-done.6 = bf16[1,256,256]{2,1,0:T(8,128)(2,1)S(1)} copy-done((bf16[1,256,256]{2,1,0:T(8,128)(2,1)S(1)}, bf16[1,256,256]{2,1,0:T(8,128)(2,1)}, u32[]{:S(2)}) %copy-start.6) | copy-done | bytes 131096
  7.1 0.0 copy-start.7
  7.1 0.9 %copy-done.7 = bf16[1,256,256]{2,1,0:T(8,128)(2,1)S(1)} copy-done((bf16[1,256,256]{2,1,0:T(8,128)(2,1)S(1)}, bf16[1,256,256]{2,1,0:T(8,128)(2,1)}, u32[]{:S(2)}) %copy-start.7) | copy-done | bytes 131096
  8.0 0.0 copy-start.8
  8.0 0.7 copy-done.8
  8.7 0.0 copy-start.9
  8.7 0.7 copy-done.9
  9.3 0.0 copy-start.10
  9.3 0.7 copy-done.10
  10.0 63.9 %propagate.1 = (f32[256,256]{1,0:T(8,128)S(1)}, f32[256,256]{1,0:T(8,128)S(1)}) custom-call(f32[256,256]{1,0:T(8,128)S(1)} %copy-done, f32[256,256]{1,0:T(8,128)S(1)} %copy-done.1, bf16[1,256,256]{2,1,0:T(8,128)(2,1)S(1)} %copy-done.2, bf16[1,256,256]{2,1,0:T(8,128)(2,1)S(1)} %copy-done.3, bf16[1,256,256]{2,1,0:T(8,128)(2,1)S(1)} %copy-done.4, ...), custom_call_target="tpu_custom_call" | custom-call | tf_op jit(solution)/shard_map/propagate/pallas_call | solution.py:324
  73.9 0.7 copy.15
  74.6 0.7 copy.16
Async XLA Ops:
  0.6 1.0 %copy-start = (f32[256,256]{1,0:T(8,128)S(1)}, f32[256,256]{1,0:T(8,128)}, u32[]{:S(2)}) copy-start(f32[256,256]{1,0:T(8,128)} %rho_re.1) | copy-start | bytes 786436
  1.6 0.9 %copy-start.1 = (f32[256,256]{1,0:T(8,128)S(1)}, f32[256,256]{1,0:T(8,128)}, u32[]{:S(2)}) copy-start(f32[256,256]{1,0:T(8,128)} %rho_im.1) | copy-start | bytes 786436
  2.5 0.9 %copy-start.2 = (bf16[1,256,256]{2,1,0:T(8,128)(2,1)S(1)}, bf16[1,256,256]{2,1,0:T(8,128)(2,1)}, u32[]{:S(2)}) copy-start(bf16[1,256,256]{2,1,0:T(8,128)(2,1)} %diag_re.1) | copy-start | bytes 393220
  3.4 0.9 %copy-start.3 = (bf16[1,256,256]{2,1,0:T(8,128)(2,1)S(1)}, bf16[1,256,256]{2,1,0:T(8,128)(2,1)}, u32[]{:S(2)}) copy-start(bf16[1,256,256]{2,1,0:T(8,128)(2,1)} %diag_im.1) | copy-start | bytes 393220
  4.3 0.9 %copy-start.4 = (bf16[1,256,256]{2,1,0:T(8,128)(2,1)S(1)}, bf16[1,256,256]{2,1,0:T(8,128)(2,1)}, u32[]{:S(2)}) copy-start(bf16[1,256,256]{2,1,0:T(8,128)(2,1)} %coup_re.1) | copy-start | bytes 393220
  5.2 0.9 %copy-start.5 = (bf16[1,256,256]{2,1,0:T(8,128)(2,1)S(1)}, bf16[1,256,256]{2,1,0:T(8,128)(2,1)}, u32[]{:S(2)}) copy-start(bf16[1,256,256]{2,1,0:T(8,128)(2,1)} %coup_im.1) | copy-start | bytes 393220
  6.2 0.9 %copy-start.6 = (bf16[1,256,256]{2,1,0:T(8,128)(2,1)S(1)}, bf16[1,256,256]{2,1,0:T(8,128)(2,1)}, u32[]{:S(2)}) copy-start(bf16[1,256,256]{2,1,0:T(8,128)(2,1)} %inj_re.1) | copy-start | bytes 393220
  7.1 0.9 %copy-start.7 = (bf16[1,256,256]{2,1,0:T(8,128)(2,1)S(1)}, bf16[1,256,256]{2,1,0:T(8,128)(2,1)}, u32[]{:S(2)}) copy-start(bf16[1,256,256]{2,1,0:T(8,128)(2,1)} %inj_im.1) | copy-start | bytes 393220
  8.0 0.7 copy-start.8
  8.7 0.7 copy-start.9
  9.3 0.7 copy-start.10

commit v2 on v1

v2 whole, which is shorter than its diff:
```python
import jax
import jax.numpy as jnp
from jax import lax
from jax.experimental import pallas as pl
from jax.experimental.pallas import tpu as pltpu
from jax.sharding import PartitionSpec as P

S = 256
LEADS = 4
PIECE = 16

step_scale = 0.25
coeff_zero = 0.7652
coeff_one = 0.8801
coeff_two = 0.2298

BF = jnp.bfloat16
F32 = jnp.float32
MESH = pl.DeviceIdType.MESH


def nn(a, b):
    return jnp.dot(a, b, preferred_element_type=F32)


def nt(a, b):
    return lax.dot_general(a, b, (((1,), (1,)), ((), ())), preferred_element_type=F32)


def pick(key, table):
    out = jnp.int32(table[-1])
    for i in range(len(table) - 1):
        out = jnp.where(key == i, jnp.int32(table[i]), out)
    return out


STEP_OF = ((1, 0, 2, 4, 4, 4, 4, 3), (3, 1, 4, 4, 4, 4, 2, 0))
OFF_OF = ((1, 0, 2, 7), (7, 1, 6, 0))

HALF = 128


def kernel(
    rho_re_hbm, rho_im_hbm, diag_re_hbm, diag_im_hbm, coup_re_hbm, coup_im_hbm, inj_re_hbm, inj_im_hbm,
    deph_hbm, lead_slice_hbm, lead_slot_hbm,
    out_re_hbm, out_im_hbm,
    rho, diag, coup, deph, lead_slice, lead_slot, result,
    field, part, far, own, right, q_out, q_in,
    kmine, kall, dmat, lpiece, kcol, lrow, crow, cprev, l_part, l_far, rate, acc, phi, fix,
    in_sem, out_sem,
    y_send, y_recv, z_send, z_recv, c_send, c_recv, q_send, q_recv,
    k_send, k_recv, ay_send, ay_recv, a_send, a_recv, b_send, b_recv, h_send, h_recv, s_send, s_recv,
):
    r = lax.axis_index("row")
    c = lax.axis_index("col")
    core = c % 2
    y_lo = r % 2
    partner = r + 1 - 2 * y_lo
    relay = (r + 2 - 4 * y_lo + 16) % 16
    c_mate = c + 1 - 2 * core
    c_out = c - 1 + 2 * core
    has_out = jnp.logical_and(c_out >= 0, c_out < 16)

    def dev(a, b):
        return {"row": a, "col": b}

    def local(src, dst, i):
        return pltpu.make_async_copy(src, dst, in_sem.at[i])

    rows16 = pl.ds(pl.multiple_of(r * PIECE, PIECE), PIECE)
    loads = [
        local(inj_re_hbm.at[0, rows16, :], kmine.at[0], 0),
        local(inj_im_hbm.at[0, rows16, :], kmine.at[1], 1),
        local(rho_re_hbm, rho.at[0], 2),
        local(rho_im_hbm, rho.at[1], 3),
        local(coup_re_hbm.at[0], coup.at[0], 4),
        local(coup_im_hbm.at[0], coup.at[1], 5),
        local(diag_re_hbm.at[0], diag.at[0], 6),
        local(diag_im_hbm.at[0], diag.at[1], 7),
        local(deph_hbm, deph, 8),
        local(lead_slice_hbm, lead_slice, 9),
        local(lead_slot_hbm, lead_slot, 10),
    ]
    for load in loads:
        load.start()

    zr, xc, hc = r // 2, (c // 2) % 4, c // 8
    sources = []
    for j in range(2):
        q = (r + 16 - j) % 16
        step = (xc + 4 - (q // 2) % 4) % 4
        zp = (zr + pick(step, OFF_OF[j])) % 8
        yp = jnp.where(hc == q // 8, y_lo, 1 - y_lo)
        sources.append((2 * zp + yp, q))
    targets = []
    for j in range(2):
        row_to = (c + j) % 16
        step = pick((r // 2 + 8 - row_to // 2) % 8, STEP_OF[j])
        x_to = ((c // 2) % 4 + step) % 4
        h_to = jnp.where(y_lo == row_to % 2, c // 8, 1 - c // 8)
        targets.append((step < 4, row_to, 8 * h_to + 2 * x_to))

    barrier = pltpu.get_barrier_semaphore()

    def greet(a, b):
        pl.semaphore_signal(barrier, inc=1, device_id=dev(a, b), device_id_type=MESH)

    @pl.loop(0, 16)
    def _(i):
        @pl.when(jnp.logical_or(i != r, c != r))
        def _():
            greet(i, r)

    for p, q in sources:
        greet(p, q)

    @pl.loop(1, 8)
    def _(i):
        greet(r, (c + 2 * i) % 16)
        greet((r + 2 * i) % 16, c)

    @pl.when(has_out)
    def _():
        greet(r, c_out)

    greet(partner, c)
    greet(r, c_mate)

    for load in loads[:4]:
        load.wait()
    kslot = 8 * core + c // 2
    kall[kslot] = kmine[...]

    def halves(ref, value_re, value_im):
        for p, value in enumerate((value_re, value_im)):
            for h in range(2):
                ref[h, p] = value[:, h * HALF : (h + 1) * HALF]

    halves(field.at[0], rho[0].astype(BF), rho[1].astype(BF))

    @pl.when(c == 15)
    def _():
        right[...] = jnp.zeros_like(right)

    @pl.when(c == 0)
    def _():
        q_in[...] = jnp.zeros_like(q_in)

    own_piece = jnp.where(r == c, 1, 0)
    sends_h = sum(jnp.where(t[0], 2, 0) for t in targets)
    pl.semaphore_wait(barrier, 2 + jnp.where(has_out, 1, 0) + 14 + 16 - own_piece + sends_h)

    def remote(src, dst, ss, rs, to):
        return pltpu.make_async_remote_copy(
            src_ref=src, dst_ref=dst, send_sem=ss, recv_sem=rs, device_id=to, device_id_type=MESH
        )

    def drain(ref, sem):
        pltpu.make_async_copy(ref, ref, sem).wait()

    def row_copies(g):
        ys, zs = [], []
        for h in range(2):
            for p in range(2):
                i = 4 * g + 2 * h + p
                ys.append(remote(field.at[g, h, p], part.at[g, h, p], y_send.at[i], y_recv.at[i], dev(partner, c)))
                zs.append(remote(part.at[g, h, p], far.at[g, h, p], z_send.at[i], z_recv.at[i], dev(relay, c)))
        return ys, zs

    def col_copies(g, src):
        cs = remote(src, right.at[g], c_send.at[g], c_recv.at[g], dev(r, c - 1))
        qs = remote(q_out.at[g], q_in.at[g], q_send.at[g], q_recv.at[g], dev(r, c + 1))
        return cs, qs

    def full(ref):
        return (
            jnp.concatenate([ref[0, 0], ref[1, 0]], axis=1),
            jnp.concatenate([ref[0, 1], ref[1, 1]], axis=1),
        )

    @pl.loop(1, 8)
    def _(i):
        remote(kmine, kall.at[kslot], k_send, k_recv, dev(r, (c + 2 * i) % 16)).start()

    ys, zs = row_copies(0)
    for y in ys:
        y.start()
    cs, qs = col_copies(0, field.at[0])

    @pl.when(c > 0)
    def _():
        cs.start()

    for load in loads[4:]:
        load.wait()

    for j, (on, row_to, col_to) in enumerate(targets):
        land = (crow, cprev)[j]

        @pl.when(on)
        def _():
            remote(coup.at[0], land.at[0], h_send.at[2 * j], h_recv.at[j], dev(row_to, col_to)).start()
            remote(coup.at[1], land.at[1], h_send.at[2 * j + 1], h_recv.at[j], dev(row_to, col_to + 1)).start()

    def product_right(g, fr, fi):
        cr, ci = coup[0], coup[1]
        q_out[g, 0] = (nt(fr, ci) - nt(fi, cr)).astype(BF)
        q_out[g, 1] = (nt(fr, cr) + nt(fi, ci)).astype(BF)

    fr, fi = full(field.at[0])
    product_right(0, fr, fi)

    @pl.when(c < 15)
    def _():
        qs.start()

    gr = diag[0].astype(F32)
    gi = diag[1].astype(F32)
    dmat[0] = (0.5 * (gr + gr.T)).astype(BF)
    dmat[1] = (0.5 * (gi - gi.T)).astype(BF)

    def forward(y, z):
        y.wait_recv()
        z.start()

    forward(ys[0], zs[0])
    drain(kall.at[pl.ds(0, 7)], k_recv)
    eight = pl.ds(8 * core, 8)
    swap = remote(kall.at[eight], kall.at[eight], s_send.at[3], s_recv.at[3], dev(r, c_mate))
    swap.start()
    forward(ys[1], zs[1])

    g_rows = deph[pl.ds(pl.multiple_of(r * S, S), S)].reshape(1, S)
    g_cols = deph[pl.ds(pl.multiple_of(c * S, S), S)].reshape(1, S)
    wide = jnp.broadcast_to(g_rows, (S, S)).T + jnp.broadcast_to(g_cols, (S, S))
    ii = lax.broadcasted_iota(jnp.int32, (S, S), 0) + r * S
    jj = lax.broadcasted_iota(jnp.int32, (S, S), 1) + c * S
    rate[...] = jnp.where(ii == jj, 0.0, 0.5 * wide)

    swap.wait_recv()
    sum_re = jnp.zeros((PIECE, S), F32)
    sum_im = jnp.zeros((PIECE, S), F32)
    for l in range(LEADS):
        slot = lead_slot[l]
        block = kall[8 * (slot % 2) + slot // 2].astype(F32)
        hit = jnp.where(lead_slice[l] == c, 1.0, 0.0)
        sum_re = sum_re + hit * block[0]
        sum_im = sum_im + hit * block[1]
    lpiece[0] = (dmat[1, rows16, :].astype(F32) - sum_re).astype(BF)
    lpiece[1] = (-dmat[0, rows16, :].astype(F32) - sum_im).astype(BF)
    kcol[r, 0] = sum_re.astype(BF)
    kcol[r, 1] = sum_im.astype(BF)

    @pl.loop(0, 16)
    def _(i):
        @pl.when(jnp.logical_or(r != c, i != c))
        def _():
            remote(lpiece.at[i % 2], lrow.at[i % 2, r], b_send, b_recv, dev(c, i)).start()

    @pl.when(r == c)
    def _():
        lrow[core, r] = lpiece[core]

    ay = remote(kcol.at[r], kcol.at[r], ay_send, ay_recv, dev(partner, c))
    ay.start()
    forward(ys[2], zs[2])
    forward(ys[3], zs[3])

    ay.wait_recv()
    pair = pl.ds(r - y_lo, 2)

    @pl.loop(1, 8)
    def _(i):
        remote(kcol.at[pair], kcol.at[pair], a_send, a_recv, dev((r + 2 * i) % 16, c)).start()

    def local_terms(own_re, own_im, fr, fi):
        dr, di = dmat[0], dmat[1]
        acc[0] = -rate[...] * own_re - nn(fr, di) - nn(fi, dr)
        acc[1] = -rate[...] * own_im + nn(fr, dr) - nn(fi, di)

    local_terms(rho[0], rho[1], fr, fi)

    shares = []
    for j, land in enumerate((crow, cprev)):
        pltpu.make_async_copy(land.at[0], land.at[0], h_recv.at[j]).wait()
        s = remote(land.at[core], land.at[core], s_send.at[j], s_recv.at[j], dev(r, c_mate))
        s.start()
        shares.append(s)

    def add_right(g):
        @pl.when(c < 15)
        def _():
            cs.wait_recv()

        nr, ni = full(right.at[g])
        cr, ci = coup[0], coup[1]
        acc[0] -= nn(nr, ci) + nn(ni, cr)
        acc[1] += nn(nr, cr) - nn(ni, ci)

    def add_q(g):
        @pl.when(c > 0)
        def _():
            qs.wait_recv()

        acc[0] += q_in[g, 0].astype(F32)
        acc[1] += q_in[g, 1].astype(F32)

    add_right(0)
    add_q(0)

    shares[0].wait_recv()
    shares[1].wait_recv()
    has_prior = jnp.where(r > 0, 1.0, 0.0).astype(BF)
    minus_prior = jnp.where(r > 0, -1.0, 0.0).astype(BF)
    minus_next = jnp.where(r < 15, -1.0, 0.0).astype(BF)

    def place(to_prior, to_next):
        to_prior[0] = has_prior * cprev[1]
        to_prior[1] = minus_prior * cprev[0]
        to_next[0] = minus_next * crow[1].T
        to_next[1] = minus_next * crow[0].T

    @pl.when(y_lo == 0)
    def _():
        place(l_far, l_part)

    @pl.when(y_lo == 1)
    def _():
        place(l_part, l_far)

    def left(lr, li, fr, fi):
        return nn(lr, fr) - nn(li, fi), nn(lr, fi) + nn(li, fr)

    def add_left(h, lr, li, fr, fi):
        more = left(lr, li, fr, fi)
        span = slice(h * HALF, (h + 1) * HALF)
        acc[0, :, span] += more[0]
        acc[1, :, span] += more[1]

    for h in range(2):
        add_left(h, l_part[0], l_part[1], part[0, h, 0], part[0, h, 1])

    @pl.when(r == c)
    def _():
        drain(lrow.at[0, pl.ds(0, 15)], b_recv)

    @pl.when(r != c)
    def _():
        drain(lrow.at[0], b_recv)

    s = remote(lrow.at[core], lrow.at[core], s_send.at[2], s_recv.at[2], dev(r, c_mate))
    s.start()
    shares.append(s)
    s.wait_recv()
    lr, li = lrow[0].reshape(S, S), lrow[1].reshape(S, S)
    more = left(lr, li, fr, fi)
    acc[0] += more[0]
    acc[1] += more[1]

    ys2, zs2 = row_copies(1)
    for h in range(2):
        zs[2 * h].wait_recv()
        zs[2 * h + 1].wait_recv()
        more = left(l_far[0], l_far[1], far[0, h, 0], far[0, h, 1])
        span = slice(h * HALF, (h + 1) * HALF)
        for p in range(2):
            value = step_scale * (acc[p, :, span] + more[p])
            phi[p, :, span] = value
            field[1, h, p] = value.astype(BF)
            ys2[2 * h + p].start()

    drain(kcol.at[pl.ds(0, 14)], a_recv)

    def lead_right(fr, fi):
        kr, ki = kcol[:, 0].reshape(S, S), kcol[:, 1].reshape(S, S)
        return step_scale * (nt(fr, kr) + nt(fi, ki)), step_scale * (nt(fi, kr) - nt(fr, ki))

    less = lead_right(fr, fi)
    phi[0] = phi[0] - less[0]
    phi[1] = phi[1] - less[1]
    halves(own, phi[0].astype(BF), phi[1].astype(BF))
    cs0, qs0 = cs, qs
    cs, qs = col_copies(1, own)

    @pl.when(c > 0)
    def _():
        cs.start()

    gr, gi = full(own)
    product_right(1, gr, gi)

    @pl.when(c < 15)
    def _():
        qs.start()

    fix[0], fix[1] = lead_right(*full(part.at[0]))
    forward(ys2[0], zs2[0])
    fix[2], fix[3] = lead_right(*full(far.at[0]))
    forward(ys2[1], zs2[1])
    local_terms(phi[0], phi[1], gr, gi)
    less = lead_right(gr, gi)
    more = left(lr, li, gr, gi)
    for p in range(2):
        acc[p] += more[p] - less[p] * (1.0 / step_scale)
    forward(ys2[2], zs2[2])
    forward(ys2[3], zs2[3])

    def corrected(ref, k, h):
        span = slice(h * HALF, (h + 1) * HALF)
        return [(ref[1, h, p].astype(F32) - fix[k + p, :, span]).astype(BF) for p in range(2)]

    @pl.when(c < 15)
    def _():
        cs.wait_recv()

    nr, ni = full(right.at[1])
    cr, ci = coup[0], coup[1]
    acc[0] -= nn(nr, ci) + nn(ni, cr)
    acc[1] += nn(nr, cr) - nn(ni, ci)

    @pl.when(c > 0)
    def _():
        qs.wait_recv()

    for p in range(2):
        acc[p] += q_in[1, p].astype(F32)
    for h in range(2):
        add_left(h, l_part[0], l_part[1], *corrected(part, 0, h))
    for p in range(2):
        acc[p] = (
            (coeff_zero - coeff_two) * rho[p] + coeff_one * phi[p] + (2.0 * coeff_two * step_scale) * acc[p]
        )
    stores = []
    for h in range(2):
        zs2[2 * h].wait_recv()
        zs2[2 * h + 1].wait_recv()
        more = left(l_far[0], l_far[1], *corrected(far, 2, h))
        span = slice(h * HALF, (h + 1) * HALF)
        for p in range(2):
            result[p, :, span] = acc[p, :, span] + (2.0 * coeff_two * step_scale) * more[p]
            out = (out_re_hbm, out_im_hbm)[p]
            store = pltpu.make_async_copy(result.at[p, :, pl.ds(h * HALF, HALF)], out.at[:, pl.ds(h * HALF, HALF)], out_sem.at[2 * h + p])
            store.start()
            stores.append(store)

    for copies in (ys, zs, ys2, zs2, shares, (swap, ay)):
        for one in copies:
            one.wait_send()

    @pl.when(c > 0)
    def _():
        cs0.wait_send()
        cs.wait_send()

    @pl.when(c < 15)
    def _():
        qs0.wait_send()
        qs.wait_send()

    drain(kall.at[pl.ds(0, 7)], k_send)
    drain(kcol.at[pl.ds(0, 14)], a_send)

    @pl.when(r == c)
    def _():
        drain(lrow.at[0, pl.ds(0, 15)], b_send)

    @pl.when(r != c)
    def _():
        drain(lrow.at[0], b_send)

    for j, (on, row_to, col_to) in enumerate(targets):
        @pl.when(on)
        def _():
            pltpu.make_async_copy(coup.at[0], coup.at[0], h_send.at[2 * j]).wait()
            pltpu.make_async_copy(coup.at[1], coup.at[1], h_send.at[2 * j + 1]).wait()

    for store in stores:
        store.wait()


def shards(*args):
    hbm = pl.BlockSpec(memory_space=pl.ANY)
    dma = pltpu.SemaphoreType.DMA

    def blocks(*n):
        return pltpu.VMEM((*n, S, S), BF)

    def split(*n):
        return pltpu.VMEM((*n, 2, 2, S, HALF), BF)

    pieces = (16, 2, PIECE, S)
    return pl.pallas_call(
        kernel,
        name="propagate",
        out_shape=[jax.ShapeDtypeStruct((S, S), F32)] * 2,
        in_specs=[hbm] * 11,
        out_specs=[hbm] * 2,
        scratch_shapes=[
            pltpu.VMEM((2, S, S), F32), blocks(2), blocks(2), pltpu.VMEM((16 * S,), F32),
            pltpu.SMEM((LEADS,), jnp.int32), pltpu.SMEM((LEADS,), jnp.int32), pltpu.VMEM((2, S, S), F32),
            split(2), split(2), split(2), split(), split(2), blocks(2, 2), blocks(2, 2),
            pltpu.VMEM((2, PIECE, S), BF), pltpu.VMEM(pieces, BF), blocks(2),
            pltpu.VMEM((2, PIECE, S), BF), pltpu.VMEM(pieces, BF), pltpu.VMEM((2, 16, PIECE, S), BF),
            blocks(2), blocks(2), blocks(2), blocks(2),
            pltpu.VMEM((S, S), F32), pltpu.VMEM((2, S, S), F32), pltpu.VMEM((2, S, S), F32), pltpu.VMEM((4, S, S), F32),
            dma((11,)), dma((4,)),
            dma((8,)), dma((8,)), dma((8,)), dma((8,)), dma((2,)), dma((2,)), dma((2,)), dma((2,)),
            dma, dma, dma, dma, dma, dma, dma, dma, dma((4,)), dma((2,)), dma((4,)), dma((4,)),
        ],
        compiler_params=pltpu.CompilerParams(
            collective_id=0, has_side_effects=True, vmem_limit_bytes=60 << 20
        ),
    )(*args)


def solution(mesh):
    return jax.shard_map(
        shards,
        mesh=mesh,
        in_specs=(
            P("row", "col"), P("row", "col"),
            P("col", None, None), P("col", None, None), P("col", None, None), P("col", None, None),
            P("col", None, None), P("col", None, None),
            P(), P(), P(),
        ),
        out_specs=(P("row", "col"), P("row", "col")),
        check_vma=False,
    )
```

time: 75.6 us -> 66.1 us (0.87)
  local copies, waits for them, and re-layouts: 10.7 us -> 2.42 us
  Pallas kernels: 63.9 us -> 62.9 us
    unnamed x24 -> x4, local copies, waits for them, and re-layouts: 10.7 us -> 2.42 us
    pallas_call x1, Pallas kernels: 63.9 us -> 62.9 us  [shards(): pl.pallas_call(kernel, name='propagate', out_shape=[jax.ShapeDtypeStruct(...]
where the time goes in v2:
time: 66.1 us; the launch traced here: 65.9 us
  Pallas kernels  62.9 us (95%)
  local copies, waits for them, and re-layouts  2.42 us (4%)
    pallas_call x1, Pallas kernels, shards(): pl.pallas_call(kernel, name='propagate', out_shape=[jax.ShapeDtypeStruct(...  62.9 us
    unnamed x4, local copies, waits for them, and re-layouts  2.42 us

profile of v2, /device:TPU:1, one launch (start us, length us, event | category | flops | bytes accessed | tf_op | source)
XLA Modules:
  0.0 65.9 jit_solution(7598458930775818839)
XLA Ops:
  0.6 62.9 %propagate.1 = (f32[256,256]{1,0:T(8,128)}, f32[256,256]{1,0:T(8,128)}) custom-call(f32[256,256]{1,0:T(8,128)} %rho_re_hbm.1, f32[256,256]{1,0:T(8,128)} %rho_im_hbm.1, bf16[1,256,256]{2,1,0:T(8,128)(2,1)} %diag_re_hbm.1, bf16[1,256,256]{2,1,0:T(8,128)(2,1)} %diag_im_hbm.1, bf16[1,256,256]{2,1,0:T(8,128)(2,1)} %coup_re_hbm.1, ...), custom_call_target="tpu_custom_call" | custom-call | tf_op jit(solution)/shard_map/propagate/pallas_call | solution.py:492
  63.5 0.0 copy-start
  63.5 1.7 %copy.15 = f32[256,256]{1,0:T(8,128)} copy(f32[256,256]{1,0:T(8,128)} %get-tuple-element.4) | data formatting | bytes 524288
  65.2 0.0 copy-done
  65.2 0.7 %copy.16 = f32[256,256]{1,0:T(8,128)} copy(f32[256,256]{1,0:T(8,128)S(1)} %copy-done) | data formatting | bytes 524288
Async XLA Ops:
  63.5 1.7 %copy-start = (f32[256,256]{1,0:T(8,128)S(1)}, f32[256,256]{1,0:T(8,128)}, u32[]{:S(2)}) copy-start(f32[256,256]{1,0:T(8,128)} %get-tuple-element.5) | copy-start | bytes 786436

commit v3 on v2

--- a/solution.py
+++ b/solution.py
@@ -27,16 +27,6 @@
     return lax.dot_general(a, b, (((1,), (1,)), ((), ())), preferred_element_type=F32)
 
 
-def pick(key, table):
-    out = jnp.int32(table[-1])
-    for i in range(len(table) - 1):
-        out = jnp.where(key == i, jnp.int32(table[i]), out)
-    return out
-
-
-STEP_OF = ((1, 0, 2, 4, 4, 4, 4, 3), (3, 1, 4, 4, 4, 4, 2, 0))
-OFF_OF = ((1, 0, 2, 7), (7, 1, 6, 0))
-
 HALF = 128
 
 
@@ -44,12 +34,13 @@
     rho_re_hbm, rho_im_hbm, diag_re_hbm, diag_im_hbm, coup_re_hbm, coup_im_hbm, inj_re_hbm, inj_im_hbm,
     deph_hbm, lead_slice_hbm, lead_slot_hbm,
     out_re_hbm, out_im_hbm,
-    rho, diag, coup, deph, lead_slice, lead_slot, result,
+    rho, diag, coup, inj, deph, lead_slice, lead_slot, result,
     field, part, far, own, right, q_out, q_in,
-    kmine, kall, dmat, lpiece, kcol, lrow, crow, cprev, l_part, l_far, rate, acc, phi, fix,
+    kmine, kall, dmat, kcol, msum, m_in, rs_in, y_sum, y_in, lrow, crow, cprev, l_part, l_far, rate, acc, phi, fix,
     in_sem, out_sem,
     y_send, y_recv, z_send, z_recv, c_send, c_recv, q_send, q_recv,
-    k_send, k_recv, ay_send, ay_recv, a_send, a_recv, b_send, b_recv, h_send, h_recv, s_send, s_recv,
+    k_send, k_recv, ay_send, ay_recv, a_send, a_recv, h_send, h_recv, s_send, s_recv,
+    m_send, m_recv, rs_send, rs_recv, hi_send, hi_recv, ag_send, ag_recv,
 ):
     r = lax.axis_index("row")
     c = lax.axis_index("col")
@@ -80,39 +71,57 @@
         local(deph_hbm, deph, 8),
         local(lead_slice_hbm, lead_slice, 9),
         local(lead_slot_hbm, lead_slot, 10),
+        local(inj_re_hbm.at[0], inj.at[0], 11),
+        local(inj_im_hbm.at[0], inj.at[1], 12),
     ]
     for load in loads:
         load.start()
 
-    zr, xc, hc = r // 2, (c // 2) % 4, c // 8
-    sources = []
+    z, x, hi = r // 2, (c // 2) % 4, c // 8
+    way = 1 - 2 * core
+
+    def col(hi, x, core):
+        return 8 * hi + 2 * ((x + 8) % 4) + core
+
+    z_side = (z + 8 + 1 - 2 * y_lo) % 8
+    rings = []
     for j in range(2):
         q = (r + 16 - j) % 16
-        step = (xc + 4 - (q // 2) % 4) % 4
-        zp = (zr + pick(step, OFF_OF[j])) % 8
-        yp = jnp.where(hc == q // 8, y_lo, 1 - y_lo)
-        sources.append((2 * zp + yp, q))
-    targets = []
+        dist = ((x - (q // 2) % 4) * way + 8) % 4
+        near = hi == q // 8
+        start_far = jnp.where(core == 0, r + 1 - 2 * y_lo, 2 * z_side + 1 - y_lo)
+        rings.append(dict(
+            q=q,
+            enters=jnp.logical_and(dist == 0, jnp.logical_not(near)),
+            first=jnp.logical_and(dist == 1, near),
+            start_far=start_far,
+            passes=jnp.logical_and(dist < 3, jnp.logical_or(dist > 0, jnp.logical_not(near))),
+        ))
+    roots = []
     for j in range(2):
-        row_to = (c + j) % 16
-        step = pick((r // 2 + 8 - row_to // 2) % 8, STEP_OF[j])
-        x_to = ((c // 2) % 4 + step) % 4
-        h_to = jnp.where(y_lo == row_to % 2, c // 8, 1 - c // 8)
-        targets.append((step < 4, row_to, 8 * h_to + 2 * x_to))
+        to = (c + j) % 16
+        to_lo = to % 2
+        other = (to // 2 + 8 + 1 - 2 * to_lo) % 8
+        roots.append(dict(
+            to=to,
+            own=r == to,
+            far_re=r == to + 1 - 2 * to_lo,
+            far_im=r == 2 * other + 1 - to_lo,
+        ))
 
     barrier = pltpu.get_barrier_semaphore()
 
     def greet(a, b):
         pl.semaphore_signal(barrier, inc=1, device_id=dev(a, b), device_id_type=MESH)
 
-    @pl.loop(0, 16)
-    def _(i):
-        @pl.when(jnp.logical_or(i != r, c != r))
-        def _():
-            greet(i, r)
-
-    for p, q in sources:
-        greet(p, q)
+    for ring in rings:
+        @pl.when(ring["enters"])
+        def _():
+            greet(ring["start_far"], ring["q"])
+
+        @pl.when(ring["first"])
+        def _():
+            greet(r, ring["q"])
 
     @pl.loop(1, 8)
     def _(i):
@@ -146,9 +155,10 @@
     def _():
         q_in[...] = jnp.zeros_like(q_in)
 
-    own_piece = jnp.where(r == c, 1, 0)
-    sends_h = sum(jnp.where(t[0], 2, 0) for t in targets)
-    pl.semaphore_wait(barrier, 2 + jnp.where(has_out, 1, 0) + 14 + 16 - own_piece + sends_h)
+    sends_h = sum(
+        jnp.where(t["own"], 2, 0) + jnp.where(t["far_re"], 1, 0) + jnp.where(t["far_im"], 1, 0) for t in roots
+    )
+    pl.semaphore_wait(barrier, 2 + jnp.where(has_out, 1, 0) + 14 + sends_h)
 
     def remote(src, dst, ss, rs, to):
         return pltpu.make_async_remote_copy(
@@ -178,29 +188,87 @@
             jnp.concatenate([ref[0, 1], ref[1, 1]], axis=1),
         )
 
+    ys, zs = row_copies(0)
+    for y in ys:
+        y.start()
+    for load in loads[4:]:
+        load.wait()
+
+    gr = diag[0].astype(F32)
+    gi = diag[1].astype(F32)
+    dmat[0] = (0.5 * (gr + gr.T)).astype(BF)
+    dmat[1] = (0.5 * (gi - gi.T)).astype(BF)
+
+    mine = jnp.where(r == c, 1.0, 0.0)
+    hits = jnp.float32(0.0)
+    for l in range(LEADS):
+        hits = hits + jnp.where(jnp.logical_and(lead_slice[l] == r, lead_slot[l] == c), 1.0, 0.0)
+    share_re = mine * dmat[1].astype(F32) - hits * inj[0].astype(F32)
+    share_im = -mine * dmat[0].astype(F32) - hits * inj[1].astype(F32)
+    msum[0] = share_re.astype(BF).reshape(4, 64, S)
+    msum[1] = share_im.astype(BF).reshape(4, 64, S)
+    to_mate = remote(msum.at[1 - core], m_in, m_send, m_recv, dev(r, c_mate))
+    to_mate.start()
+
+    lands = (crow, cprev)
+    h_copies = []
+    for j, root in enumerate(roots):
+        for u in range(2):
+            rows = pl.ds(128 * u, 128)
+            i = 2 * j + u
+
+            def send(kind, on, p, to):
+                copy = remote(coup.at[p, rows], lands[j].at[p, rows], h_send.at[6 * i + kind], h_recv.at[i], to)
+                h_copies.append((on, copy))
+
+                @pl.when(on)
+                def _():
+                    copy.start()
+
+            to = root["to"]
+            send(0, root["own"], 0, dev(to, col(hi, x + 1, 0)))
+            send(1, root["own"], 1, dev(to, col(hi, x - 1, 1)))
+            send(2, root["own"], 1 - core, dev(to, c_mate))
+            send(3, root["far_re"], 0, dev(to, col(1 - hi, x, 0)))
+            send(4, root["far_im"], 1, dev(to, col(1 - hi, x, 1)))
+
+        @pl.when(root["own"])
+        def _():
+            lands[j][core] = coup[core]
+
+    def pass_on(j, u):
+        rows = pl.ds(128 * u, 128)
+        i = 2 * j + u
+        place = lands[j].at[core, rows]
+        on = rings[j]["passes"]
+        copy = remote(place, place, h_send.at[6 * i + 5], h_recv.at[i], dev(r, col(hi, x + way, core)))
+        h_copies.append((on, copy))
+
+        @pl.when(on)
+        def _():
+            copy.wait_recv()
+            copy.start()
+
     @pl.loop(1, 8)
     def _(i):
         remote(kmine, kall.at[kslot], k_send, k_recv, dev(r, (c + 2 * i) % 16)).start()
 
-    ys, zs = row_copies(0)
-    for y in ys:
-        y.start()
     cs, qs = col_copies(0, field.at[0])
 
     @pl.when(c > 0)
     def _():
         cs.start()
 
-    for load in loads[4:]:
-        load.wait()
-
-    for j, (on, row_to, col_to) in enumerate(targets):
-        land = (crow, cprev)[j]
-
-        @pl.when(on)
-        def _():
-            remote(coup.at[0], land.at[0], h_send.at[2 * j], h_recv.at[j], dev(row_to, col_to)).start()
-            remote(coup.at[1], land.at[1], h_send.at[2 * j + 1], h_recv.at[j], dev(row_to, col_to + 1)).start()
+    to_mate.wait_recv()
+    msum[core] = (msum[core].astype(F32) + m_in[...].astype(F32)).astype(BF)
+    scatter, gather = [], []
+    for i in range(1, 4):
+        peer = dev(r, col(hi, x + i, core))
+        scatter.append(remote(msum.at[core, (x + i) % 4], rs_in.at[i - 1], rs_send.at[i - 1], rs_recv.at[i - 1], peer))
+        quarter = lrow.at[core, x]
+        gather.append(remote(quarter, quarter, ag_send.at[i - 1], ag_recv.at[i - 1], peer))
+    for copy in scatter:
+        copy.start()
 
     def product_right(g, fr, fi):
         cr, ci = coup[0], coup[1]
@@ -214,21 +282,22 @@
     def _():
         qs.start()
 
-    gr = diag[0].astype(F32)
-    gi = diag[1].astype(F32)
-    dmat[0] = (0.5 * (gr + gr.T)).astype(BF)
-    dmat[1] = (0.5 * (gi - gi.T)).astype(BF)
-
     def forward(y, z):
         y.wait_recv()
         z.start()
 
     forward(ys[0], zs[0])
-    drain(kall.at[pl.ds(0, 7)], k_recv)
-    eight = pl.ds(8 * core, 8)
-    swap = remote(kall.at[eight], kall.at[eight], s_send.at[3], s_recv.at[3], dev(r, c_mate))
-    swap.start()
+    pass_on(0, 0)
+    for copy in scatter:
+        copy.wait_recv()
+    total = msum[core, x].astype(F32)
+    for i in range(3):
+        total = total + rs_in[i].astype(F32)
+    y_sum[...] = total.astype(BF)
+    cross = remote(y_sum, y_in, hi_send, hi_recv, dev(r, (c + 8) % 16))
+    cross.start()
     forward(ys[1], zs[1])
+    pass_on(0, 1)
 
     g_rows = deph[pl.ds(pl.multiple_of(r * S, S), S)].reshape(1, S)
     g_cols = deph[pl.ds(pl.multiple_of(c * S, S), S)].reshape(1, S)
@@ -236,6 +305,19 @@
     ii = lax.broadcasted_iota(jnp.int32, (S, S), 0) + r * S
     jj = lax.broadcasted_iota(jnp.int32, (S, S), 1) + c * S
     rate[...] = jnp.where(ii == jj, 0.0, 0.5 * wide)
+
+    drain(kall.at[pl.ds(0, 7)], k_recv)
+    eight = pl.ds(8 * core, 8)
+    swap = remote(kall.at[eight], kall.at[eight], s_send.at[3], s_recv.at[3], dev(r, c_mate))
+    swap.start()
+    forward(ys[2], zs[2])
+    pass_on(1, 0)
+    cross.wait_recv()
+    lrow[core, x] = (y_sum[...].astype(F32) + y_in[...].astype(F32)).astype(BF)
+    for copy in gather:
+        copy.start()
+    forward(ys[3], zs[3])
+    pass_on(1, 1)
 
     swap.wait_recv()
     sum_re = jnp.zeros((PIECE, S), F32)
@@ -246,32 +328,10 @@
         hit = jnp.where(lead_slice[l] == c, 1.0, 0.0)
         sum_re = sum_re + hit * block[0]
         sum_im = sum_im + hit * block[1]
-    lpiece[0] = (dmat[1, rows16, :].astype(F32) - sum_re).astype(BF)
-    lpiece[1] = (-dmat[0, rows16, :].astype(F32) - sum_im).astype(BF)
     kcol[r, 0] = sum_re.astype(BF)
     kcol[r, 1] = sum_im.astype(BF)
-
-    @pl.loop(0, 16)
-    def _(i):
-        @pl.when(jnp.logical_or(r != c, i != c))
-        def _():
-            remote(lpiece.at[i % 2], lrow.at[i % 2, r], b_send, b_recv, dev(c, i)).start()
-
-    @pl.when(r == c)
-    def _():
-        lrow[core, r] = lpiece[core]
-
     ay = remote(kcol.at[r], kcol.at[r], ay_send, ay_recv, dev(partner, c))
     ay.start()
-    forward(ys[2], zs[2])
-    forward(ys[3], zs[3])
-
-    ay.wait_recv()
-    pair = pl.ds(r - y_lo, 2)
-
-    @pl.loop(1, 8)
-    def _(i):
-        remote(kcol.at[pair], kcol.at[pair], a_send, a_recv, dev((r + 2 * i) % 16, c)).start()
 
     def local_terms(own_re, own_im, fr, fi):
         dr, di = dmat[0], dmat[1]
@@ -281,11 +341,29 @@
     local_terms(rho[0], rho[1], fr, fi)
 
     shares = []
-    for j, land in enumerate((crow, cprev)):
-        pltpu.make_async_copy(land.at[0], land.at[0], h_recv.at[j]).wait()
-        s = remote(land.at[core], land.at[core], s_send.at[j], s_recv.at[j], dev(r, c_mate))
-        s.start()
-        shares.append(s)
+    for j, land in enumerate(lands):
+        for u in range(2):
+            @pl.when(jnp.logical_and(c != rings[j]["q"], jnp.logical_not(rings[j]["passes"])))
+            def _():
+                part_of = land.at[0, pl.ds(128 * u, 128)]
+                pltpu.make_async_copy(part_of, part_of, h_recv.at[2 * j + u]).wait()
+
+        share = remote(land.at[core], land.at[core], s_send.at[j], s_recv.at[j], dev(r, c_mate))
+        share.start()
+        shares.append(share)
+
+    ay.wait_recv()
+    pair = pl.ds(r - y_lo, 2)
+
+    @pl.loop(1, 8)
+    def _(i):
+        remote(kcol.at[pair], kcol.at[pair], a_send, a_recv, dev((r + 2 * i) % 16, c)).start()
+
+    for copy in gather:
+        copy.wait_recv()
+    share = remote(lrow.at[core], lrow.at[core], s_send.at[2], s_recv.at[2], dev(r, c_mate))
+    share.start()
+    shares.append(share)
 
     def add_right(g):
         @pl.when(c < 15)
@@ -340,18 +418,7 @@
     for h in range(2):
         add_left(h, l_part[0], l_part[1], part[0, h, 0], part[0, h, 1])
 
-    @pl.when(r == c)
-    def _():
-        drain(lrow.at[0, pl.ds(0, 15)], b_recv)
-
-    @pl.when(r != c)
-    def _():
-        drain(lrow.at[0], b_recv)
-
-    s = remote(lrow.at[core], lrow.at[core], s_send.at[2], s_recv.at[2], dev(r, c_mate))
-    s.start()
-    shares.append(s)
-    s.wait_recv()
+    shares[2].wait_recv()
     lr, li = lrow[0].reshape(S, S), lrow[1].reshape(S, S)
     more = left(lr, li, fr, fi)
     acc[0] += more[0]
@@ -443,7 +510,7 @@
             store.start()
             stores.append(store)
 
-    for copies in (ys, zs, ys2, zs2, shares, (swap, ay)):
+    for copies in (ys, zs, ys2, zs2, shares, scatter, gather, (swap, ay, to_mate, cross)):
         for one in copies:
             one.wait_send()
 
@@ -460,19 +527,10 @@
     drain(kall.at[pl.ds(0, 7)], k_send)
     drain(kcol.at[pl.ds(0, 14)], a_send)
 
-    @pl.when(r == c)
-    def _():
-        drain(lrow.at[0, pl.ds(0, 15)], b_send)
-
-    @pl.when(r != c)
-    def _():
-        drain(lrow.at[0], b_send)
-
-    for j, (on, row_to, col_to) in enumerate(targets):
+    for on, copy in h_copies:
         @pl.when(on)
         def _():
-            pltpu.make_async_copy(coup.at[0], coup.at[0], h_send.at[2 * j]).wait()
-            pltpu.make_async_copy(coup.at[1], coup.at[1], h_send.at[2 * j + 1]).wait()
+            copy.wait_send()
 
     for store in stores:
         store.wait()
@@ -487,6 +545,9 @@
 
     def split(*n):
         return pltpu.VMEM((*n, 2, 2, S, HALF), BF)
+
+    def quarters(*n):
+        return pltpu.VMEM((*n, 64, S), BF)
 
     pieces = (16, 2, PIECE, S)
     return pl.pallas_call(
@@ -496,16 +557,17 @@
         in_specs=[hbm] * 11,
         out_specs=[hbm] * 2,
         scratch_shapes=[
-            pltpu.VMEM((2, S, S), F32), blocks(2), blocks(2), pltpu.VMEM((16 * S,), F32),
+            pltpu.VMEM((2, S, S), F32), blocks(2), blocks(2), blocks(2), pltpu.VMEM((16 * S,), F32),
             pltpu.SMEM((LEADS,), jnp.int32), pltpu.SMEM((LEADS,), jnp.int32), pltpu.VMEM((2, S, S), F32),
             split(2), split(2), split(2), split(), split(2), blocks(2, 2), blocks(2, 2),
             pltpu.VMEM((2, PIECE, S), BF), pltpu.VMEM(pieces, BF), blocks(2),
-            pltpu.VMEM((2, PIECE, S), BF), pltpu.VMEM(pieces, BF), pltpu.VMEM((2, 16, PIECE, S), BF),
+            pltpu.VMEM(pieces, BF), quarters(2, 4), quarters(4), quarters(3), quarters(), quarters(), quarters(2, 4),
             blocks(2), blocks(2), blocks(2), blocks(2),
             pltpu.VMEM((S, S), F32), pltpu.VMEM((2, S, S), F32), pltpu.VMEM((2, S, S), F32), pltpu.VMEM((4, S, S), F32),
-            dma((11,)), dma((4,)),
+            dma((13,)), dma((4,)),
             dma((8,)), dma((8,)), dma((8,)), dma((8,)), dma((2,)), dma((2,)), dma((2,)), dma((2,)),
-            dma, dma, dma, dma, dma, dma, dma, dma, dma((4,)), dma((2,)), dma((4,)), dma((4,)),
+            dma, dma, dma, dma, dma, dma, dma((24,)), dma((4,)), dma((4,)), dma((4,)),
+            dma, dma, dma((3,)), dma((3,)), dma, dma, dma((3,)), dma((3,)),
         ],
         compiler_params=pltpu.CompilerParams(
             collective_id=0, has_side_effects=True, vmem_limit_bytes=60 << 20

time: 66.1 us -> 54.7 us (0.83)
  Pallas kernels: 62.9 us -> 51.5 us
    pallas_call x1, Pallas kernels: 62.9 us -> 51.5 us  [shards(): pl.pallas_call(kernel, name='propagate', out_shape=[jax.ShapeDtypeStruct(...]
where the time goes in v3:
time: 54.7 us; the launch traced here: 54.6 us
  Pallas kernels  51.5 us (94%)
  local copies, waits for them, and re-layouts  2.42 us (4%)
  between operations  0.65 us (1%)
    pallas_call x1, Pallas kernels, shards(): pl.pallas_call(kernel, name='propagate', out_shape=[jax.ShapeDtypeStruct(...  51.5 us
    unnamed x4, local copies, waits for them, and re-layouts  2.42 us

profile of v3, /device:TPU:1, one launch (start us, length us, event | category | flops | bytes accessed | tf_op | source)
XLA Modules:
  0.0 54.6 jit_solution(17179514670209150249)
XLA Ops:
  0.6 51.5 %propagate.1 = (f32[256,256]{1,0:T(8,128)}, f32[256,256]{1,0:T(8,128)}) custom-call(f32[256,256]{1,0:T(8,128)} %rho_re_hbm.1, f32[256,256]{1,0:T(8,128)} %rho_im_hbm.1, bf16[1,256,256]{2,1,0:T(8,128)(2,1)} %diag_re_hbm.1, bf16[1,256,256]{2,1,0:T(8,128)(2,1)} %diag_im_hbm.1, bf16[1,256,256]{2,1,0:T(8,128)(2,1)} %coup_re_hbm.1, ...), custom_call_target="tpu_custom_call" | custom-call | tf_op jit(solution)/shard_map/propagate/pallas_call | solution.py:553
  52.1 0.0 copy-start
  52.1 1.7 %copy.15 = f32[256,256]{1,0:T(8,128)} copy(f32[256,256]{1,0:T(8,128)} %get-tuple-element.4) | data formatting | bytes 524288
  53.9 0.0 copy-done
  53.9 0.7 %copy.16 = f32[256,256]{1,0:T(8,128)} copy(f32[256,256]{1,0:T(8,128)S(1)} %copy-done) | data formatting | bytes 524288
Async XLA Ops:
  52.1 1.7 %copy-start = (f32[256,256]{1,0:T(8,128)S(1)}, f32[256,256]{1,0:T(8,128)}, u32[]{:S(2)}) copy-start(f32[256,256]{1,0:T(8,128)} %get-tuple-element.5) | copy-start | bytes 786436

commit v4 on v3

--- a/solution.py
+++ b/solution.py
@@ -33,11 +33,11 @@
 def kernel(
     rho_re_hbm, rho_im_hbm, diag_re_hbm, diag_im_hbm, coup_re_hbm, coup_im_hbm, inj_re_hbm, inj_im_hbm,
     deph_hbm, lead_slice_hbm, lead_slot_hbm,
-    out_re_hbm, out_im_hbm,
-    rho, diag, coup, inj, deph, lead_slice, lead_slot, result,
+    out_re, out_im,
+    rho, diag, coup, inj, deph, lead_slice, lead_slot,
     field, part, far, own, right, q_out, q_in,
     kmine, kall, dmat, kcol, msum, m_in, rs_in, y_sum, y_in, lrow, crow, cprev, l_part, l_far, rate, acc, phi, fix,
-    in_sem, out_sem,
+    in_sem,
     y_send, y_recv, z_send, z_recv, c_send, c_recv, q_send, q_recv,
     k_send, k_recv, ay_send, ay_recv, a_send, a_recv, h_send, h_recv, s_send, s_recv,
     m_send, m_recv, rs_send, rs_recv, hi_send, hi_recv, ag_send, ag_recv,
@@ -93,6 +93,7 @@
         rings.append(dict(
             q=q,
             enters=jnp.logical_and(dist == 0, jnp.logical_not(near)),
+            level=dist + jnp.where(near, 0, 1),
             first=jnp.logical_and(dist == 1, near),
             start_far=start_far,
             passes=jnp.logical_and(dist < 3, jnp.logical_or(dist > 0, jnp.logical_not(near))),
@@ -188,9 +189,13 @@
             jnp.concatenate([ref[0, 1], ref[1, 1]], axis=1),
         )
 
+    @pl.loop(1, 8)
+    def _(i):
+        remote(kmine, kall.at[kslot], k_send, k_recv, dev(r, (c + 2 * i) % 16)).start()
+
     ys, zs = row_copies(0)
-    for y in ys:
-        y.start()
+    ys[0].start()
+    ys[1].start()
     for load in loads[4:]:
         load.wait()
 
@@ -210,54 +215,7 @@
     to_mate = remote(msum.at[1 - core], m_in, m_send, m_recv, dev(r, c_mate))
     to_mate.start()
 
-    lands = (crow, cprev)
-    h_copies = []
-    for j, root in enumerate(roots):
-        for u in range(2):
-            rows = pl.ds(128 * u, 128)
-            i = 2 * j + u
-
-            def send(kind, on, p, to):
-                copy = remote(coup.at[p, rows], lands[j].at[p, rows], h_send.at[6 * i + kind], h_recv.at[i], to)
-                h_copies.append((on, copy))
-
-                @pl.when(on)
-                def _():
-                    copy.start()
-
-            to = root["to"]
-            send(0, root["own"], 0, dev(to, col(hi, x + 1, 0)))
-            send(1, root["own"], 1, dev(to, col(hi, x - 1, 1)))
-            send(2, root["own"], 1 - core, dev(to, c_mate))
-            send(3, root["far_re"], 0, dev(to, col(1 - hi, x, 0)))
-            send(4, root["far_im"], 1, dev(to, col(1 - hi, x, 1)))
-
-        @pl.when(root["own"])
-        def _():
-            lands[j][core] = coup[core]
-
-    def pass_on(j, u):
-        rows = pl.ds(128 * u, 128)
-        i = 2 * j + u
-        place = lands[j].at[core, rows]
-        on = rings[j]["passes"]
-        copy = remote(place, place, h_send.at[6 * i + 5], h_recv.at[i], dev(r, col(hi, x + way, core)))
-        h_copies.append((on, copy))
-
-        @pl.when(on)
-        def _():
-            copy.wait_recv()
-            copy.start()
-
-    @pl.loop(1, 8)
-    def _(i):
-        remote(kmine, kall.at[kslot], k_send, k_recv, dev(r, (c + 2 * i) % 16)).start()
-
     cs, qs = col_copies(0, field.at[0])
-
-    @pl.when(c > 0)
-    def _():
-        cs.start()
 
     to_mate.wait_recv()
     msum[core] = (msum[core].astype(F32) + m_in[...].astype(F32)).astype(BF)
@@ -270,6 +228,48 @@
     for copy in scatter:
         copy.start()
 
+    lands = (crow, cprev)
+    h_copies = []
+    for j, root in enumerate(roots):
+        for u in range(2):
+            rows = pl.ds(128 * u, 128)
+            i = 2 * j + u
+
+            def send(kind, on, p, to):
+                copy = remote(coup.at[p, rows], lands[j].at[p, rows], h_send.at[6 * i + kind], h_recv.at[i], to)
+                h_copies.append((on, copy))
+
+                @pl.when(on)
+                def _():
+                    copy.start()
+
+            to = root["to"]
+            send(0, root["own"], 0, dev(to, col(hi, x + 1, 0)))
+            send(1, root["own"], 1, dev(to, col(hi, x - 1, 1)))
+            send(2, root["own"], 1 - core, dev(to, c_mate))
+            send(3, root["far_re"], 0, dev(to, col(1 - hi, x, 0)))
+            send(4, root["far_im"], 1, dev(to, col(1 - hi, x, 1)))
+
+        @pl.when(root["own"])
+        def _():
+            lands[j][core] = coup[core]
+
+    onward = []
+    for j in range(2):
+        for u in range(2):
+            i = 2 * j + u
+            place = lands[j].at[core, pl.ds(128 * u, 128)]
+            copy = remote(place, place, h_send.at[6 * i + 5], h_recv.at[i], dev(r, col(hi, x + way, core)))
+            onward.append(copy)
+            h_copies.append((rings[j]["passes"], copy))
+
+    def pass_on(j, level):
+        @pl.when(jnp.logical_and(rings[j]["passes"], rings[j]["level"] == level))
+        def _():
+            for copy in onward[2 * j : 2 * j + 2]:
+                copy.wait_recv()
+                copy.start()
+
     def product_right(g, fr, fi):
         cr, ci = coup[0], coup[1]
         q_out[g, 0] = (nt(fr, ci) - nt(fi, cr)).astype(BF)
@@ -278,16 +278,20 @@
     fr, fi = full(field.at[0])
     product_right(0, fr, fi)
 
-    @pl.when(c < 15)
-    def _():
-        qs.start()
-
     def forward(y, z):
         y.wait_recv()
         z.start()
 
+    def pieces_in():
+        drain(kall.at[pl.ds(0, 7)], k_recv)
+        swap.start()
+
+    eight = pl.ds(8 * core, 8)
+    swap = remote(kall.at[eight], kall.at[eight], s_send.at[3], s_recv.at[3], dev(r, c_mate))
     forward(ys[0], zs[0])
-    pass_on(0, 0)
+    ys[2].start()
+    pieces_in()
+    pass_on(0, 1)
     for copy in scatter:
         copy.wait_recv()
     total = msum[core, x].astype(F32)
@@ -296,28 +300,18 @@
     y_sum[...] = total.astype(BF)
     cross = remote(y_sum, y_in, hi_send, hi_recv, dev(r, (c + 8) % 16))
     cross.start()
+
+    @pl.when(c > 0)
+    def _():
+        cs.start()
+
+    @pl.when(c < 15)
+    def _():
+        qs.start()
+
+    pass_on(1, 1)
     forward(ys[1], zs[1])
-    pass_on(0, 1)
-
-    g_rows = deph[pl.ds(pl.multiple_of(r * S, S), S)].reshape(1, S)
-    g_cols = deph[pl.ds(pl.multiple_of(c * S, S), S)].reshape(1, S)
-    wide = jnp.broadcast_to(g_rows, (S, S)).T + jnp.broadcast_to(g_cols, (S, S))
-    ii = lax.broadcasted_iota(jnp.int32, (S, S), 0) + r * S
-    jj = lax.broadcasted_iota(jnp.int32, (S, S), 1) + c * S
-    rate[...] = jnp.where(ii == jj, 0.0, 0.5 * wide)
-
-    drain(kall.at[pl.ds(0, 7)], k_recv)
-    eight = pl.ds(8 * core, 8)
-    swap = remote(kall.at[eight], kall.at[eight], s_send.at[3], s_recv.at[3], dev(r, c_mate))
-    swap.start()
-    forward(ys[2], zs[2])
-    pass_on(1, 0)
-    cross.wait_recv()
-    lrow[core, x] = (y_sum[...].astype(F32) + y_in[...].astype(F32)).astype(BF)
-    for copy in gather:
-        copy.start()
-    forward(ys[3], zs[3])
-    pass_on(1, 1)
+    ys[3].start()
 
     swap.wait_recv()
     sum_re = jnp.zeros((PIECE, S), F32)
@@ -332,6 +326,31 @@
     kcol[r, 1] = sum_im.astype(BF)
     ay = remote(kcol.at[r], kcol.at[r], ay_send, ay_recv, dev(partner, c))
     ay.start()
+    pass_on(0, 2)
+    forward(ys[2], zs[2])
+    pass_on(1, 2)
+    ay.wait_recv()
+    pair = pl.ds(r - y_lo, 2)
+
+    @pl.loop(1, 8)
+    def _(i):
+        remote(kcol.at[pair], kcol.at[pair], a_send, a_recv, dev((r + 2 * i) % 16, c)).start()
+
+    forward(ys[3], zs[3])
+    cross.wait_recv()
+    lrow[core, x] = (y_sum[...].astype(F32) + y_in[...].astype(F32)).astype(BF)
+    for copy in gather:
+        copy.start()
+
+    pass_on(0, 3)
+    pass_on(1, 3)
+
+    g_rows = deph[pl.ds(pl.multiple_of(r * S, S), S)].reshape(1, S)
+    g_cols = deph[pl.ds(pl.multiple_of(c * S, S), S)].reshape(1, S)
+    wide = jnp.broadcast_to(g_rows, (S, S)).T + jnp.broadcast_to(g_cols, (S, S))
+    ii = lax.broadcasted_iota(jnp.int32, (S, S), 0) + r * S
+    jj = lax.broadcasted_iota(jnp.int32, (S, S), 1) + c * S
+    rate[...] = jnp.where(ii == jj, 0.0, 0.5 * wide)
 
     def local_terms(own_re, own_im, fr, fi):
         dr, di = dmat[0], dmat[1]
@@ -351,13 +370,6 @@
         share = remote(land.at[core], land.at[core], s_send.at[j], s_recv.at[j], dev(r, c_mate))
         share.start()
         shares.append(share)
-
-    ay.wait_recv()
-    pair = pl.ds(r - y_lo, 2)
-
-    @pl.loop(1, 8)
-    def _(i):
-        remote(kcol.at[pair], kcol.at[pair], a_send, a_recv, dev((r + 2 * i) % 16, c)).start()
 
     for copy in gather:
         copy.wait_recv()
@@ -495,20 +507,16 @@
         add_left(h, l_part[0], l_part[1], *corrected(part, 0, h))
     for p in range(2):
         acc[p] = (
-            (coeff_zero - coeff_two) * rho[p] + coeff_one * phi[p] + (2.0 * coeff_two * step_scale) * acc[p]
+            coeff_one * phi[p] + (2.0 * coeff_two * step_scale) * acc[p]
         )
-    stores = []
     for h in range(2):
         zs2[2 * h].wait_recv()
         zs2[2 * h + 1].wait_recv()
         more = left(l_far[0], l_far[1], *corrected(far, 2, h))
         span = slice(h * HALF, (h + 1) * HALF)
         for p in range(2):
-            result[p, :, span] = acc[p, :, span] + (2.0 * coeff_two * step_scale) * more[p]
-            out = (out_re_hbm, out_im_hbm)[p]
-            store = pltpu.make_async_copy(result.at[p, :, pl.ds(h * HALF, HALF)], out.at[:, pl.ds(h * HALF, HALF)], out_sem.at[2 * h + p])
-            store.start()
-            stores.append(store)
+            out = (out_re, out_im)[p]
+            out[:, span] = acc[p, :, span] + (2.0 * coeff_two * step_scale) * more[p]
 
     for copies in (ys, zs, ys2, zs2, shares, scatter, gather, (swap, ay, to_mate, cross)):
         for one in copies:
@@ -532,9 +540,6 @@
         def _():
             copy.wait_send()
 
-    for store in stores:
-        store.wait()
-
 
 def shards(*args):
     hbm = pl.BlockSpec(memory_space=pl.ANY)
@@ -550,21 +555,21 @@
         return pltpu.VMEM((*n, 64, S), BF)
 
     pieces = (16, 2, PIECE, S)
-    return pl.pallas_call(
+    outs = pl.pallas_call(
         kernel,
         name="propagate",
         out_shape=[jax.ShapeDtypeStruct((S, S), F32)] * 2,
         in_specs=[hbm] * 11,
-        out_specs=[hbm] * 2,
+        out_specs=[pl.BlockSpec(memory_space=pltpu.VMEM)] * 2,
         scratch_shapes=[
             pltpu.VMEM((2, S, S), F32), blocks(2), blocks(2), blocks(2), pltpu.VMEM((16 * S,), F32),
-            pltpu.SMEM((LEADS,), jnp.int32), pltpu.SMEM((LEADS,), jnp.int32), pltpu.VMEM((2, S, S), F32),
+            pltpu.SMEM((LEADS,), jnp.int32), pltpu.SMEM((LEADS,), jnp.int32),
             split(2), split(2), split(2), split(), split(2), blocks(2, 2), blocks(2, 2),
             pltpu.VMEM((2, PIECE, S), BF), pltpu.VMEM(pieces, BF), blocks(2),
             pltpu.VMEM(pieces, BF), quarters(2, 4), quarters(4), quarters(3), quarters(), quarters(), quarters(2, 4),
             blocks(2), blocks(2), blocks(2), blocks(2),
             pltpu.VMEM((S, S), F32), pltpu.VMEM((2, S, S), F32), pltpu.VMEM((2, S, S), F32), pltpu.VMEM((4, S, S), F32),
-            dma((13,)), dma((4,)),
+            dma((13,)),
             dma((8,)), dma((8,)), dma((8,)), dma((8,)), dma((2,)), dma((2,)), dma((2,)), dma((2,)),
             dma, dma, dma, dma, dma, dma, dma((24,)), dma((4,)), dma((4,)), dma((4,)),
             dma, dma, dma((3,)), dma((3,)), dma, dma, dma((3,)), dma((3,)),
@@ -573,6 +578,7 @@
             collective_id=0, has_side_effects=True, vmem_limit_bytes=60 << 20
         ),
     )(*args)
+    return tuple(o + (coeff_zero - coeff_two) * a for o, a in zip(outs, args))
 
 
 def solution(mesh):

time: 54.7 us -> 50.4 us (0.921)
  the two profiles are of different devices: /device:TPU:1 before, /device:TPU:5 now
where the time goes in v4:
time: 50.4 us; the launch traced here: 50.3 us
  Pallas kernels  47.7 us (95%)
  other arithmetic  1.89 us (4%)
  between operations  0.67 us (1%)
    pallas_call x1, Pallas kernels, shards(): pl.pallas_call(kernel, name='propagate', out_shape=[jax.ShapeDtypeStruct(...  47.7 us
    add x1, other arithmetic, shards(): return tuple((o + (coeff_zero - coeff_two) * a for o, a in zip(outs, args)))  1.89 us

profile of v4, /device:TPU:5, one launch (start us, length us, event | category | flops | bytes accessed | tf_op | source)
XLA Modules:
  0.0 50.3 jit_solution(11390575708088131269)
XLA Ops:
  0.6 0.0 copy-start.1
  0.6 0.0 copy-start
  0.7 47.7 %propagate.1 = (f32[256,256]{1,0:T(8,128)}, f32[256,256]{1,0:T(8,128)}) custom-call(f32[256,256]{1,0:T(8,128)} %rho_re_hbm.1, f32[256,256]{1,0:T(8,128)} %rho_im_hbm.1, bf16[1,256,256]{2,1,0:T(8,128)(2,1)} %diag_re_hbm.1, bf16[1,256,256]{2,1,0:T(8,128)(2,1)} %diag_im_hbm.1, bf16[1,256,256]{2,1,0:T(8,128)(2,1)} %coup_re_hbm.1, ...), custom_call_target="tpu_custom_call" | custom-call | tf_op jit(solution)/shard_map/propagate/pallas_call | solution.py:558
  48.4 0.0 copy-done.1
  48.4 0.0 copy-done
  48.4 1.9 %multiply_add_fusion = (f32[256,256]{1,0:T(8,128)}, f32[256,256]{1,0:T(8,128)}) fusion(f32[256,256]{1,0:T(8,128)} %get-tuple-element.5, f32[256,256]{1,0:T(8,128)S(1)} %copy-done.1, f32[256,256]{1,0:T(8,128)} %get-tuple-element.4, f32[256,256]{1,0:T(8,128)S(1)} %copy-done), kind=kLoop, calls=%fused_computation | loop fusion | flops 262144 | bytes 1572864 | tf_op jit(solution)/shard_map/add | solution.py:581
Async XLA Ops:
  0.6 47.8 %copy-start.1 = (f32[256,256]{1,0:T(8,128)S(1)}, f32[256,256]{1,0:T(8,128)}, u32[]{:S(2)}) copy-start(f32[256,256]{1,0:T(8,128)} %rho_im_hbm.1) | copy-start | bytes 786436
  0.6 47.8 %copy-start = (f32[256,256]{1,0:T(8,128)S(1)}, f32[256,256]{1,0:T(8,128)}, u32[]{:S(2)}) copy-start(f32[256,256]{1,0:T(8,128)} %rho_re_hbm.1) | copy-start | bytes 786436

commit v5 on v4

--- a/solution.py
+++ b/solution.py
@@ -40,7 +40,7 @@
     in_sem,
     y_send, y_recv, z_send, z_recv, c_send, c_recv, q_send, q_recv,
     k_send, k_recv, ay_send, ay_recv, a_send, a_recv, h_send, h_recv, s_send, s_recv,
-    m_send, m_recv, rs_send, rs_recv, hi_send, hi_recv, ag_send, ag_recv,
+    near_sem, far_sem, m_send, m_recv, rs_send, rs_recv, hi_send, hi_recv, ag_send, ag_recv,
 ):
     r = lax.axis_index("row")
     c = lax.axis_index("col")
@@ -83,7 +83,12 @@
     def col(hi, x, core):
         return 8 * hi + 2 * ((x + 8) % 4) + core
 
-    z_side = (z + 8 + 1 - 2 * y_lo) % 8
+    def beside(z, y_lo):
+        return jnp.where(y_lo == 0, jnp.where(z < 7, z + 1, 6), jnp.where(z > 0, z - 1, 1))
+
+    z_side = beside(z, y_lo)
+    gives_far = jnp.where(y_lo == 0, z, 7 - z) < 7
+    gets_far = jnp.where(y_lo == 0, z, 7 - z) > 0
     rings = []
     for j in range(2):
         q = (r + 16 - j) % 16
@@ -102,7 +107,7 @@
     for j in range(2):
         to = (c + j) % 16
         to_lo = to % 2
-        other = (to // 2 + 8 + 1 - 2 * to_lo) % 8
+        other = beside(to // 2, to_lo)
         roots.append(dict(
             to=to,
             own=r == to,
@@ -127,7 +132,10 @@
     @pl.loop(1, 8)
     def _(i):
         greet(r, (c + 2 * i) % 16)
-        greet((r + 2 * i) % 16, c)
+
+        @pl.when(z + i < 8)
+        def _():
+            greet((r + 2 * i) % 16, c)
 
     @pl.when(has_out)
     def _():
@@ -156,10 +164,27 @@
     def _():
         q_in[...] = jnp.zeros_like(q_in)
 
+    @pl.when(jnp.logical_not(gets_far))
+    def _():
+        far[...] = jnp.zeros_like(far)
+
     sends_h = sum(
         jnp.where(t["own"], 2, 0) + jnp.where(t["far_re"], 1, 0) + jnp.where(t["far_im"], 1, 0) for t in roots
     )
-    pl.semaphore_wait(barrier, 2 + jnp.where(has_out, 1, 0) + 14 + sends_h)
+    pl.semaphore_wait(barrier, 2 + jnp.where(has_out, 1, 0) + 7 + z + sends_h)
+
+    def answer(sem, by):
+        pl.semaphore_signal(sem, inc=1, device_id=dev((r + 16 - 2 * by) % 16, c), device_id_type=MESH)
+
+    @pl.when(z > 0)
+    def _():
+        answer(near_sem, 1)
+
+    @pl.loop(2, 8)
+    def _(i):
+        @pl.when(i <= z)
+        def _():
+            answer(far_sem, i)
 
     def remote(src, dst, ss, rs, to):
         return pltpu.make_async_remote_copy(
@@ -278,9 +303,16 @@
     fr, fi = full(field.at[0])
     product_right(0, fr, fi)
 
-    def forward(y, z):
+    def forward(y, onto):
         y.wait_recv()
-        z.start()
+
+        @pl.when(gives_far)
+        def _():
+            onto.start()
+
+    @pl.when(z < 7)
+    def _():
+        pl.semaphore_wait(near_sem, 1)
 
     def pieces_in():
         drain(kall.at[pl.ds(0, 7)], k_recv)
@@ -332,6 +364,10 @@
     ay.wait_recv()
     pair = pl.ds(r - y_lo, 2)
 
+    @pl.when(z < 6)
+    def _():
+        pl.semaphore_wait(far_sem, 6 - z)
+
     @pl.loop(1, 8)
     def _(i):
         remote(kcol.at[pair], kcol.at[pair], a_send, a_recv, dev((r + 2 * i) % 16, c)).start()
@@ -438,8 +474,11 @@
 
     ys2, zs2 = row_copies(1)
     for h in range(2):
-        zs[2 * h].wait_recv()
-        zs[2 * h + 1].wait_recv()
+        @pl.when(gets_far)
+        def _():
+            zs[2 * h].wait_recv()
+            zs[2 * h + 1].wait_recv()
+
         more = left(l_far[0], l_far[1], far[0, h, 0], far[0, h, 1])
         span = slice(h * HALF, (h + 1) * HALF)
         for p in range(2):
@@ -510,16 +549,24 @@
             coeff_one * phi[p] + (2.0 * coeff_two * step_scale) * acc[p]
         )
     for h in range(2):
-        zs2[2 * h].wait_recv()
-        zs2[2 * h + 1].wait_recv()
+        @pl.when(gets_far)
+        def _():
+            zs2[2 * h].wait_recv()
+            zs2[2 * h + 1].wait_recv()
+
         more = left(l_far[0], l_far[1], *corrected(far, 2, h))
         span = slice(h * HALF, (h + 1) * HALF)
         for p in range(2):
             out = (out_re, out_im)[p]
             out[:, span] = acc[p, :, span] + (2.0 * coeff_two * step_scale) * more[p]
 
-    for copies in (ys, zs, ys2, zs2, shares, scatter, gather, (swap, ay, to_mate, cross)):
+    for copies in (ys, ys2, shares, scatter, gather, (swap, ay, to_mate, cross)):
         for one in copies:
+            one.wait_send()
+
+    @pl.when(gives_far)
+    def _():
+        for one in zs + zs2:
             one.wait_send()
 
     @pl.when(c > 0)
@@ -572,6 +619,7 @@
             dma((13,)),
             dma((8,)), dma((8,)), dma((8,)), dma((8,)), dma((2,)), dma((2,)), dma((2,)), dma((2,)),
             dma, dma, dma, dma, dma, dma, dma((24,)), dma((4,)), dma((4,)), dma((4,)),
+            pltpu.SemaphoreType.REGULAR, pltpu.SemaphoreType.REGULAR,
             dma, dma, dma((3,)), dma((3,)), dma, dma, dma((3,)), dma((3,)),
         ],
         compiler_params=pltpu.CompilerParams(

time: 50.4 us -> 46.9 us (0.931)
  the two profiles are of different devices: /device:TPU:5 before, /device:TPU:55 now
where the time goes in v5:
time: 46.9 us; the launch traced here: 46.7 us
  Pallas kernels  44.2 us (94%)
  other arithmetic  1.89 us (4%)
  between operations  0.67 us (1%)
    pallas_call x1, Pallas kernels, shards(): pl.pallas_call(kernel, name='propagate', out_shape=[jax.ShapeDtypeStruct(...  44.2 us
    add x1, other arithmetic, shards(): return tuple((o + (coeff_zero - coeff_two) * a for o, a in zip(outs, args)))  1.89 us

profile of v5, /device:TPU:55, one launch (start us, length us, event | category | flops | bytes accessed | tf_op | source)
XLA Modules:
  0.0 46.7 jit_solution(13418535739279498609)
XLA Ops:
  0.6 0.0 copy-start.1
  0.6 0.0 copy-start
  0.7 44.2 %propagate.1 = (f32[256,256]{1,0:T(8,128)}, f32[256,256]{1,0:T(8,128)}) custom-call(f32[256,256]{1,0:T(8,128)} %rho_re_hbm.1, f32[256,256]{1,0:T(8,128)} %rho_im_hbm.1, bf16[1,256,256]{2,1,0:T(8,128)(2,1)} %diag_re_hbm.1, bf16[1,256,256]{2,1,0:T(8,128)(2,1)} %diag_im_hbm.1, bf16[1,256,256]{2,1,0:T(8,128)(2,1)} %coup_re_hbm.1, ...), custom_call_target="tpu_custom_call" | custom-call | tf_op jit(solution)/shard_map/propagate/pallas_call | solution.py:605
  44.8 0.0 copy-done.1
  44.8 0.0 copy-done
  44.9 1.9 %multiply_add_fusion = (f32[256,256]{1,0:T(8,128)}, f32[256,256]{1,0:T(8,128)}) fusion(f32[256,256]{1,0:T(8,128)} %get-tuple-element.5, f32[256,256]{1,0:T(8,128)S(1)} %copy-done.1, f32[256,256]{1,0:T(8,128)} %get-tuple-element.4, f32[256,256]{1,0:T(8,128)S(1)} %copy-done), kind=kLoop, calls=%fused_computation | loop fusion | flops 262144 | bytes 1572864 | tf_op jit(solution)/shard_map/add | solution.py:629
Async XLA Ops:
  0.6 44.2 %copy-start.1 = (f32[256,256]{1,0:T(8,128)S(1)}, f32[256,256]{1,0:T(8,128)}, u32[]{:S(2)}) copy-start(f32[256,256]{1,0:T(8,128)} %rho_im_hbm.1) | copy-start | bytes 786436
  0.6 44.2 %copy-start = (f32[256,256]{1,0:T(8,128)S(1)}, f32[256,256]{1,0:T(8,128)}, u32[]{:S(2)}) copy-start(f32[256,256]{1,0:T(8,128)} %rho_re_hbm.1) | copy-start | bytes 786436

commit v6 on v5

--- a/solution.py
+++ b/solution.py
@@ -224,6 +224,32 @@
     for load in loads[4:]:
         load.wait()
 
+    lands = (crow, cprev)
+    h_copies = []
+    for j, root in enumerate(roots):
+        for u in range(2):
+            rows = pl.ds(128 * u, 128)
+            i = 2 * j + u
+
+            def send(kind, on, p, to):
+                copy = remote(coup.at[p, rows], lands[j].at[p, rows], h_send.at[6 * i + kind], h_recv.at[i], to)
+                h_copies.append((on, copy))
+
+                @pl.when(on)
+                def _():
+                    copy.start()
+
+            to = root["to"]
+            send(0, root["own"], 0, dev(to, col(hi, x + 1, 0)))
+            send(1, root["own"], 1, dev(to, col(hi, x - 1, 1)))
+            send(2, root["own"], 1 - core, dev(to, c_mate))
+            send(3, root["far_re"], 0, dev(to, col(1 - hi, x, 0)))
+            send(4, root["far_im"], 1, dev(to, col(1 - hi, x, 1)))
+
+        @pl.when(root["own"])
+        def _():
+            lands[j][core] = coup[core]
+
     gr = diag[0].astype(F32)
     gi = diag[1].astype(F32)
     dmat[0] = (0.5 * (gr + gr.T)).astype(BF)
@@ -253,32 +279,6 @@
     for copy in scatter:
         copy.start()
 
-    lands = (crow, cprev)
-    h_copies = []
-    for j, root in enumerate(roots):
-        for u in range(2):
-            rows = pl.ds(128 * u, 128)
-            i = 2 * j + u
-
-            def send(kind, on, p, to):
-                copy = remote(coup.at[p, rows], lands[j].at[p, rows], h_send.at[6 * i + kind], h_recv.at[i], to)
-                h_copies.append((on, copy))
-
-                @pl.when(on)
-                def _():
-                    copy.start()
-
-            to = root["to"]
-            send(0, root["own"], 0, dev(to, col(hi, x + 1, 0)))
-            send(1, root["own"], 1, dev(to, col(hi, x - 1, 1)))
-            send(2, root["own"], 1 - core, dev(to, c_mate))
-            send(3, root["far_re"], 0, dev(to, col(1 - hi, x, 0)))
-            send(4, root["far_im"], 1, dev(to, col(1 - hi, x, 1)))
-
-        @pl.when(root["own"])
-        def _():
-            lands[j][core] = coup[core]
-
     onward = []
     for j in range(2):
         for u in range(2):
@@ -319,7 +319,7 @@
         swap.start()
 
     eight = pl.ds(8 * core, 8)
-    swap = remote(kall.at[eight], kall.at[eight], s_send.at[3], s_recv.at[3], dev(r, c_mate))
+    swap = remote(kall.at[eight], kall.at[eight], s_send.at[4], s_recv.at[4], dev(r, c_mate))
     forward(ys[0], zs[0])
     ys[2].start()
     pieces_in()
@@ -398,18 +398,19 @@
     shares = []
     for j, land in enumerate(lands):
         for u in range(2):
+            part_of = land.at[core, pl.ds(128 * u, 128)]
+
             @pl.when(jnp.logical_and(c != rings[j]["q"], jnp.logical_not(rings[j]["passes"])))
             def _():
-                part_of = land.at[0, pl.ds(128 * u, 128)]
                 pltpu.make_async_copy(part_of, part_of, h_recv.at[2 * j + u]).wait()
 
-        share = remote(land.at[core], land.at[core], s_send.at[j], s_recv.at[j], dev(r, c_mate))
-        share.start()
-        shares.append(share)
+            share = remote(part_of, part_of, s_send.at[2 * j + u], s_recv.at[2 * j + u], dev(r, c_mate))
+            share.start()
+            shares.append(share)
 
     for copy in gather:
         copy.wait_recv()
-    share = remote(lrow.at[core], lrow.at[core], s_send.at[2], s_recv.at[2], dev(r, c_mate))
+    share = remote(lrow.at[core], lrow.at[core], s_send.at[5], s_recv.at[5], dev(r, c_mate))
     share.start()
     shares.append(share)
 
@@ -434,8 +435,8 @@
     add_right(0)
     add_q(0)
 
-    shares[0].wait_recv()
-    shares[1].wait_recv()
+    for i in range(4):
+        shares[i].wait_recv()
     has_prior = jnp.where(r > 0, 1.0, 0.0).astype(BF)
     minus_prior = jnp.where(r > 0, -1.0, 0.0).astype(BF)
     minus_next = jnp.where(r < 15, -1.0, 0.0).astype(BF)
@@ -466,7 +467,7 @@
     for h in range(2):
         add_left(h, l_part[0], l_part[1], part[0, h, 0], part[0, h, 1])
 
-    shares[2].wait_recv()
+    shares[4].wait_recv()
     lr, li = lrow[0].reshape(S, S), lrow[1].reshape(S, S)
     more = left(lr, li, fr, fi)
     acc[0] += more[0]
@@ -618,7 +619,7 @@
             pltpu.VMEM((S, S), F32), pltpu.VMEM((2, S, S), F32), pltpu.VMEM((2, S, S), F32), pltpu.VMEM((4, S, S), F32),
             dma((13,)),
             dma((8,)), dma((8,)), dma((8,)), dma((8,)), dma((2,)), dma((2,)), dma((2,)), dma((2,)),
-            dma, dma, dma, dma, dma, dma, dma((24,)), dma((4,)), dma((4,)), dma((4,)),
+            dma, dma, dma, dma, dma, dma, dma((24,)), dma((4,)), dma((6,)), dma((6,)),
             pltpu.SemaphoreType.REGULAR, pltpu.SemaphoreType.REGULAR,
             dma, dma, dma((3,)), dma((3,)), dma, dma, dma((3,)), dma((3,)),
         ],

time: 46.9 us -> 45.1 us (0.962)
  the two profiles are of different devices: /device:TPU:55 before, /device:TPU:192 now
where the time goes in v6:
time: 45.1 us; the launch traced here: 45 us
  Pallas kernels  42.4 us (94%)
  other arithmetic  1.89 us (4%)
  between operations  0.67 us (1%)
    pallas_call x1, Pallas kernels, shards(): pl.pallas_call(kernel, name='propagate', out_shape=[jax.ShapeDtypeStruct(...  42.4 us
    add x1, other arithmetic, shards(): return tuple((o + (coeff_zero - coeff_two) * a for o, a in zip(outs, args)))  1.89 us

profile of v6, /device:TPU:192, one launch (start us, length us, event | category | flops | bytes accessed | tf_op | source)
XLA Modules:
  0.0 45.0 jit_solution(14542206616758356994)
XLA Ops:
  0.6 0.0 copy-start.1
  0.6 0.0 copy-start
  0.7 42.4 %propagate.1 = (f32[256,256]{1,0:T(8,128)}, f32[256,256]{1,0:T(8,128)}) custom-call(f32[256,256]{1,0:T(8,128)} %rho_re_hbm.1, f32[256,256]{1,0:T(8,128)} %rho_im_hbm.1, bf16[1,256,256]{2,1,0:T(8,128)(2,1)} %diag_re_hbm.1, bf16[1,256,256]{2,1,0:T(8,128)(2,1)} %diag_im_hbm.1, bf16[1,256,256]{2,1,0:T(8,128)(2,1)} %coup_re_hbm.1, ...), custom_call_target="tpu_custom_call" | custom-call | tf_op jit(solution)/shard_map/propagate/pallas_call | solution.py:606
  43.1 0.0 copy-done.1
  43.1 0.0 copy-done
  43.1 1.9 %multiply_add_fusion = (f32[256,256]{1,0:T(8,128)}, f32[256,256]{1,0:T(8,128)}) fusion(f32[256,256]{1,0:T(8,128)} %get-tuple-element.5, f32[256,256]{1,0:T(8,128)S(1)} %copy-done.1, f32[256,256]{1,0:T(8,128)} %get-tuple-element.4, f32[256,256]{1,0:T(8,128)S(1)} %copy-done), kind=kLoop, calls=%fused_computation | loop fusion | flops 262144 | bytes 1572864 | tf_op jit(solution)/shard_map/add | solution.py:630
Async XLA Ops:
  0.6 42.4 %copy-start.1 = (f32[256,256]{1,0:T(8,128)S(1)}, f32[256,256]{1,0:T(8,128)}, u32[]{:S(2)}) copy-start(f32[256,256]{1,0:T(8,128)} %rho_im_hbm.1) | copy-start | bytes 786436
  0.6 42.4 %copy-start = (f32[256,256]{1,0:T(8,128)S(1)}, f32[256,256]{1,0:T(8,128)}, u32[]{:S(2)}) copy-start(f32[256,256]{1,0:T(8,128)} %rho_re_hbm.1) | copy-start | bytes 786436

commit v7 on v6

--- a/solution.py
+++ b/solution.py
@@ -219,9 +219,9 @@
         remote(kmine, kall.at[kslot], k_send, k_recv, dev(r, (c + 2 * i) % 16)).start()
 
     ys, zs = row_copies(0)
-    ys[0].start()
-    ys[1].start()
-    for load in loads[4:]:
+    for y in ys:
+        y.start()
+    for load in loads[4:6]:
         load.wait()
 
     lands = (crow, cprev)
@@ -249,6 +249,9 @@
         @pl.when(root["own"])
         def _():
             lands[j][core] = coup[core]
+
+    for load in loads[6:]:
+        load.wait()
 
     gr = diag[0].astype(F32)
     gi = diag[1].astype(F32)
@@ -321,7 +324,6 @@
     eight = pl.ds(8 * core, 8)
     swap = remote(kall.at[eight], kall.at[eight], s_send.at[4], s_recv.at[4], dev(r, c_mate))
     forward(ys[0], zs[0])
-    ys[2].start()
     pieces_in()
     pass_on(0, 1)
     for copy in scatter:
@@ -343,7 +345,6 @@
 
     pass_on(1, 1)
     forward(ys[1], zs[1])
-    ys[3].start()
 
     swap.wait_recv()
     sum_re = jnp.zeros((PIECE, S), F32)

time: 45.1 us -> 45.1 us (level)
  no operation moved by 1% of the time
where the time goes in v7:
time: 45.1 us; the launch traced here: 45 us
  Pallas kernels  42.4 us (94%)
  other arithmetic  1.89 us (4%)
  between operations  0.67 us (1%)
    pallas_call x1, Pallas kernels, shards(): pl.pallas_call(kernel, name='propagate', out_shape=[jax.ShapeDtypeStruct(...  42.4 us
    add x1, other arithmetic, shards(): return tuple((o + (coeff_zero - coeff_two) * a for o, a in zip(outs, args)))  1.89 us

profile of v7, /device:TPU:192, one launch (start us, length us, event | category | flops | bytes accessed | tf_op | source)
XLA Modules:
  0.0 45.0 jit_solution(11275109712399125791)
XLA Ops:
  0.6 0.0 copy-start.1
  0.6 0.0 copy-start
  0.7 42.4 %propagate.1 = (f32[256,256]{1,0:T(8,128)}, f32[256,256]{1,0:T(8,128)}) custom-call(f32[256,256]{1,0:T(8,128)} %rho_re_hbm.1, f32[256,256]{1,0:T(8,128)} %rho_im_hbm.1, bf16[1,256,256]{2,1,0:T(8,128)(2,1)} %diag_re_hbm.1, bf16[1,256,256]{2,1,0:T(8,128)(2,1)} %diag_im_hbm.1, bf16[1,256,256]{2,1,0:T(8,128)(2,1)} %coup_re_hbm.1, ...), custom_call_target="tpu_custom_call" | custom-call | tf_op jit(solution)/shard_map/propagate/pallas_call | solution.py:607
  43.1 0.0 copy-done.1
  43.1 0.0 copy-done
  43.1 1.9 %multiply_add_fusion = (f32[256,256]{1,0:T(8,128)}, f32[256,256]{1,0:T(8,128)}) fusion(f32[256,256]{1,0:T(8,128)} %get-tuple-element.5, f32[256,256]{1,0:T(8,128)S(1)} %copy-done.1, f32[256,256]{1,0:T(8,128)} %get-tuple-element.4, f32[256,256]{1,0:T(8,128)S(1)} %copy-done), kind=kLoop, calls=%fused_computation | loop fusion | flops 262144 | bytes 1572864 | tf_op jit(solution)/shard_map/add | solution.py:631
Async XLA Ops:
  0.6 42.4 %copy-start.1 = (f32[256,256]{1,0:T(8,128)S(1)}, f32[256,256]{1,0:T(8,128)}, u32[]{:S(2)}) copy-start(f32[256,256]{1,0:T(8,128)} %rho_im_hbm.1) | copy-start | bytes 786436
  0.6 42.4 %copy-start = (f32[256,256]{1,0:T(8,128)S(1)}, f32[256,256]{1,0:T(8,128)}, u32[]{:S(2)}) copy-start(f32[256,256]{1,0:T(8,128)} %rho_re_hbm.1) | copy-start | bytes 786436
